TPU v7x, 32 devices: a whole 2x2x4 slice. The times are simulated.
32 devices in a mesh: space: 4 (over x, core), frame: 8 (over z, y).
Axes of the slice: x: 2, y: 2, z: 4, core: 2. Of those that a mesh axis runs over, the one named last changes fastest.
Arguments:
- latent: bfloat16 [8, 2048, 1024], P('frame', 'space'), may hold values from -6 to 6
- cond: float32 [3, 1024], replicated, may hold values from -3 to 3
- w_qkv: bfloat16 [1024, 3072], replicated
- w_out: bfloat16 [1024, 1024], replicated, may hold values from -0.1875 to 0.1875
- slot: int32 [2048], P('space'), may hold values from 0 to 511, as said below
- neighbours: int32 [16, 4], P('space'), may hold values from 0 to 15, as said below
- counts: int32 [16], P('space'), may hold values from 1 to 4
Outputs:
- updated: bfloat16 [8, 2048, 1024], P('frame', 'space')
Inputs may be any that keep to these rules, and one draw needn't show every extreme that they name: `slot`: each aligned group of 512 entries is a permutation of its range. `neighbours`: row b lists distinct blocks (b + o) mod 16 with -4 <= o <= 4, the first being b itself.
All inputs are finite; a program needn't handle non-finite values.
Results may differ from a plain program's by a relative error of at most 0.0052.
Values may be sent and summed in bfloat16 or wider, within the bound.
A program may use at most 64 MiB of HBM per device.

v0:
```python
import jax
import jax.numpy as jnp
from jax import lax
from jax.sharding import PartitionSpec as P

HEADS = 8
MAXNB = 4


def with_halo(cells, sides, width):
    for axis, dim in sides:
        count = lax.axis_size(axis)
        head = lax.slice_in_dim(cells, 0, width, axis=dim)
        tail = lax.slice_in_dim(cells, cells.shape[dim] - width, cells.shape[dim], axis=dim)
        cells = jnp.concatenate(
            [
                lax.ppermute(tail, axis, [(i, (i + 1) % count) for i in range(count)]),
                cells,
                lax.ppermute(head, axis, [((i + 1) % count, i) for i in range(count)]),
            ],
            axis=dim,
        )
    return cells


def softmax_last(scores):
    top = jnp.max(scores, axis=-1, keepdims=True)
    expo = jnp.exp(scores - top)
    return expo / jnp.sum(expo, axis=-1, keepdims=True)


def body(latent, cond, w_qkv, w_out, slot, neighbours, counts):
    tokens = latent.shape[1]
    width = latent.shape[2]
    blocks = neighbours.shape[0]
    block_len = tokens // blocks
    half = width // 2
    head_dim = width // HEADS
    sheads = HEADS // 2
    scale = 1.0 / jnp.sqrt(jnp.float32(head_dim))
    frame_total = lax.axis_size("frame")
    clip_len = min(8, frame_total)
    rows = latent[0].astype(jnp.float32)
    centred = rows - jnp.mean(rows, axis=-1, keepdims=True)
    normed = centred * lax.rsqrt(jnp.mean(centred * centred, axis=-1, keepdims=True) + 1e-06)
    modulated = (normed * (1.0 + cond[1]) + cond[0]).astype(jnp.bfloat16)
    projected = jnp.dot(modulated, w_qkv, preferred_element_type=jnp.float32).astype(jnp.bfloat16)
    query_sp = jnp.take(projected[:, :half], slot, axis=0)
    keyval = jnp.take(
        jnp.concatenate(
            [projected[:, width : width + half], projected[:, 2 * width : 2 * width + half]], axis=1
        ),
        slot,
        axis=0,
    )
    window = with_halo(keyval, (("space", 0),), tokens)
    total_blocks = blocks * lax.axis_size("space")
    first_block = (lax.axis_index("space") - 1) * blocks
    local_ids = jnp.mod(neighbours - first_block, total_blocks)
    valid = jnp.arange(MAXNB, dtype=jnp.int32)[None, :] < counts[:, None]
    query_blocks = query_sp.reshape(blocks, block_len, sheads, head_dim)
    keys = window[:, :half].reshape(3 * tokens, sheads, head_dim)
    vals = window[:, half:].reshape(3 * tokens, sheads, head_dim)
    scores = (
        jnp.einsum("jqhd,khd->jhqk", query_blocks, keys, preferred_element_type=jnp.float32) * scale
    )
    allowed = jnp.any(
        (local_ids[:, :, None] == jnp.arange(3 * blocks, dtype=jnp.int32)[None, None, :])
        & valid[:, :, None],
        axis=1,
    )
    keep = jnp.repeat(allowed, block_len, axis=1)[:, None, None, :]
    weights = softmax_last(jnp.where(keep, scores, -jnp.inf)).astype(jnp.bfloat16)
    attended = jnp.einsum("jhqk,khd->jqhd", weights, vals, preferred_element_type=jnp.float32)
    block_out = attended.astype(jnp.bfloat16).reshape(tokens, half)
    spatial = jnp.zeros_like(block_out).at[slot].set(block_out)
    t_query = projected[:, half:width]
    t_key = projected[:, width + half : 2 * width]
    t_val = projected[:, 2 * width + half :]
    per_dest = tokens // frame_total
    stacked = jnp.concatenate([t_query, t_key, t_val], axis=1).reshape(
        1, frame_total, per_dest, 3 * half
    )
    group = lax.all_to_all(stacked, "frame", split_axis=1, concat_axis=0, tiled=True)
    frame_count = group.shape[0]
    count = group.shape[2]
    parts = group.reshape(frame_count, count, 3, sheads, head_dim)
    t_scores = (
        jnp.einsum(
            "fnhd,gnhd->nhfg", parts[:, :, 0], parts[:, :, 1], preferred_element_type=jnp.float32
        )
        * scale
    )
    clip_of = jnp.arange(frame_count, dtype=jnp.int32) // clip_len
    same_clip = clip_of[:, None] == clip_of[None, :]
    t_weights = softmax_last(jnp.where(same_clip[None, None], t_scores, -jnp.inf))
    result = jnp.einsum(
        "nhfg,gnhd->fnhd",
        t_weights,
        parts[:, :, 2].astype(jnp.float32),
        precision=lax.Precision.HIGHEST,
        preferred_element_type=jnp.float32,
    )
    mixed_frames = result.astype(jnp.bfloat16).reshape(frame_count, 1, count, half)
    temporal = lax.all_to_all(
        mixed_frames, "frame", split_axis=0, concat_axis=1, tiled=True
    ).reshape(tokens, half)
    joined = jnp.concatenate([spatial, temporal], axis=1)
    mixed = jnp.dot(joined, w_out, preferred_element_type=jnp.float32)
    return (rows + cond[2] * mixed).astype(jnp.bfloat16)[None]


def solution(mesh):
    in_specs = (P("frame", "space", None), P(), P(), P(), P("space"), P("space", None), P("space"))
    out_specs = P("frame", "space", None)
    return jax.shard_map(body, mesh=mesh, in_specs=in_specs, out_specs=out_specs, check_vma=False)
```

profile of v0, /device:TPU:0, one launch (start us, length us, event | category | flops | bytes accessed | tf_op | source)
XLA Modules:
  0.0 97.9 jit_solution(9464918873207642789)
XLA Ops:
  1.6 1.4 %convert_reduce_fusion = f32[512]{0:T(512)S(1)} fusion(bf16[1,512,1024]{2,1,0:T(8,128)(2,1)} %param.7), kind=kLoop, calls=%fused_computation.14 | loop fusion | flops 1048064 | bytes 1050624 | tf_op jit(solution)/shard_map/reduce_sum | solution.py:44
  3.0 1.6 %fusion.10 = f32[512]{0:T(512)S(1)} fusion(bf16[1,512,1024]{2,1,0:T(8,128)(2,1)} %param.7, f32[512]{0:T(512)S(1)} %broadcast_multiply_fusion), kind=kLoop, calls=%fused_computation.20 | loop fusion | flops 2096640 | bytes 1052672 | tf_op jit(solution)/shard_map/reduce_sum | solution.py:45
  4.7 6.7 %convolution_convert_fusion = bf16[512,3072]{1,0:T(8,128)(2,1)S(1)} fusion(bf16[1024,3072]{1,0:T(8,128)(2,1)} %param.9, bf16[1,512,1024]{2,1,0:T(8,128)(2,1)S(1)} %copy-done.2, f32[1024]{0:T(1024)S(1)} %bitcast.99, f32[1024]{0:T(1024)S(1)} %bitcast.100, f32[512]{0:T(512)S(1)} %add_rsqrt_fusion, f32[512]{0:T(512)S(1)} %broadcast_multiply_fusion), kind=kOutput, calls=%fused_computation.12 | convolution fusion | flops 3225944064 | bytes 10498048 | tf_op jit(solution)/shard_map/dot_general | solution.py:47
  11.5 1.4 %fusion.53 = (bf16[512,512]{1,0:T(8,128)(2,1)}, bf16[512,512]{1,0:T(8,128)(2,1)}, bf16[512,512]{1,0:T(8,128)(2,1)}, bf16[512,512]{1,0:T(8,128)(2,1)}, bf16[512,5...) fusion(bf16[512,3072]{1,0:T(8,128)(2,1)S(1)} %convolution_convert_fusion), kind=kLoop, calls=%fused_computation.85 | loop fusion | bytes 6291456 | tf_op jit(solution)/shard_map/slice | solution.py:48
  13.0 2.8 %gather_fusion = bf16[512,1024]{1,0:T(8,128)(2,1)} fusion(bf16[512,1024]{1,0:T(8,128)(2,1)S(1)} %pad_maximum_fusion.2, s32[1024]{0:T(1024)S(1)} %pad_clamp_fusion), kind=kCustom, calls=%fused_computation | custom fusion | bytes 2099200 | tf_op jit(solution)/shard_map/jit(_take)/gather | solution.py:49
  15.8 2.5 %broadcast_select_fusion = bf16[512,1024]{1,0:T(8,128)(2,1)} fusion(bf16[512,1024]{1,0:T(8,128)(2,1)} %gather_fusion, pred[512]{0:T(512)(128)(4,1)S(1)} %compare_and_fusion), kind=kLoop, calls=%fused_computation.44 | loop fusion | flops 524288 | bytes 2097664 | tf_op jit(solution)/shard_map/jit(_take)/select_n | solution.py:49
  18.3 2.4 %collective-permute-start.1 = (bf16[512,1024]{1,0:T(8,128)(2,1)}, bf16[512,1024]{1,0:T(8,128)(2,1)}, u32[]{:S(2)}, u32[]{:S(2)}) collective-permute-start(bf16[512,1024]{1,0:T(8,128)(2,1)} %broadcast_select_fusion), channel_id=1, source_target_pairs={{8,0},{16,8},{24,16},{0,24},{9,1},{17,9},{25,17},{1,25},{10,2},{18... | collective-permute-start | bytes 3145736 | tf_op jit(solution)/shard_map/ppermute | solution.py:19
  21.9 6.0 %all-to-all-start = ((bf16[1,8,64,1536]{3,2,0,1:T(8,128)(2,1)}), bf16[1,8,64,1536]{3,2,0,1:T(8,128)(2,1)}, u32[]{:S(2)}, u32[]{:S(2)}) async-start(bf16[1,8,64,1536]{3,2,0,1:T(8,128)(2,1)} %bitcast.93), calls=%async_computation | async-start | bytes 3145728 | tf_op jit(solution)/shard_map/all_to_all | solution.py:84
  28.2 2.0 %gather_fusion.1 = bf16[512,512]{1,0:T(8,128)(2,1)S(1)} fusion(bf16[512,512]{1,0:T(8,128)(2,1)S(1)} %copy-done.1, s32[1024]{0:T(1024)S(1)} %pad_clamp_fusion), kind=kCustom, calls=%fused_computation.1 | custom fusion | bytes 1050624 | tf_op jit(solution)/shard_map/jit(_take)/gather | solution.py:48
  30.4 14.1 %collective-permute-done.1 = bf16[512,1024]{1,0:T(8,128)(2,1)} collective-permute-done((bf16[512,1024]{1,0:T(8,128)(2,1)}, bf16[512,1024]{1,0:T(8,128)(2,1)}, u32[]{:S(2)}, u32[]{:S(2)}) %collective-permute-start.1) | collective-permute-done | bytes 1048608 | tf_op jit(solution)/shard_map/ppermute | solution.py:19
  45.5 2.0 %pad_maximum_fusion = bf16[1536,1024]{1,0:T(8,128)(2,1)S(1)} fusion(bf16[512,1024]{1,0:T(8,128)(2,1)} %collective-permute-done.1, bf16[512,1024]{1,0:T(8,128)(2,1)} %broadcast_select_fusion, bf16[512,1024]{1,0:T(8,128)(2,1)} %collective-permute-done), kind=kLoop, calls=%fused_computation.13 | loop fusion | flops 9437184 | bytes 6291456 | tf_op jit(solution)/shard_map/concatenate | solution.py:15
  47.6 1.9 %fusion.54 = (bf16[1536,512]{1,0:T(8,128)(2,1)}, bf16[1536,512]{1,0:T(8,128)(2,1)}) fusion(bf16[1536,1024]{1,0:T(8,128)(2,1)S(1)} %pad_maximum_fusion), kind=kLoop, calls=%fused_computation.86 | loop fusion | bytes 6291456 | tf_op jit(solution)/shard_map/slice | solution.py:62
  49.4 2.6 %copy.37 = bf16[1536,512]{0,1:T(8,128)(2,1)} copy(bf16[1536,512]{1,0:T(8,128)(2,1)} %get-tuple-element.11) | data formatting | bytes 3145728 | tf_op jit(solution)/shard_map/slice | solution.py:62
  52.1 2.6 %copy.36 = bf16[1536,512]{0,1:T(8,128)(2,1)} copy(bf16[1536,512]{1,0:T(8,128)(2,1)} %get-tuple-element.12) | data formatting | bytes 3145728 | tf_op jit(solution)/shard_map/slice | solution.py:63
  54.7 9.3 %fusion.58 = (f32[4,4,128]{2,0,1:T(4,128)S(1)}, f32[4,4,128,1536]{2,3,0,1:T(8,128)}) fusion(pred[4,1536]{1,0:T(4,128)(4,1)S(1)} %bitcast.97, bf16[1536,4,128,1]{0,2,3,1:T(8,128)(2,1)} %bitcast.96, bf16[4,128,4,128]{3,2,1,0:T(4,128)(2,1)S(1)} %gather.12, pred[4,128]{1,0:T(4,128)(4,1)S(1)} %fusion.64), kind=kOutput, calls=%fused_computation.90 | convolution fusion | flops 818152960 | bytes 14694912 | tf_op jit(solution)/shard_map/sub | solution.py:28
  64.0 1.9 %all-to-all-done = bf16[1,8,64,1536]{3,2,0,1:T(8,128)(2,1)} async-done(((bf16[1,8,64,1536]{3,2,0,1:T(8,128)(2,1)}), bf16[1,8,64,1536]{3,2,0,1:T(8,128)(2,1)}, u32[]{:S(2)}, u32[]{:S(2)}) %all-to-all-start) | async-done | bytes 1572896 | tf_op jit(solution)/shard_map/all_to_all | solution.py:84
  65.8 4.0 %reshape.137 = bf16[8,64,3,4,128]{4,3,2,1,0:T(4,128)(2,1)} reshape(bf16[1,8,64,1536]{3,2,0,1:T(8,128)(2,1)} %all-to-all-done) | data formatting | bytes 3145728 | tf_op jit(solution)/shard_map/reshape | solution.py:87
  69.8 2.0 %fusion.55 = (bf16[8,64,1,4,128]{4,3,2,1,0:T(4,128)(2,1)S(1)}, bf16[8,64,1,4,128]{4,3,2,1,0:T(4,128)(2,1)S(1)}, bf16[8,64,1,4,128]{4,3,2,1,0:T(4,128)(2,1)S(1)}) fusion(bf16[8,64,3,4,128]{4,3,2,1,0:T(4,128)(2,1)} %reshape.137), kind=kLoop, calls=%fused_computation.87 | loop fusion | bytes 3145728 | tf_op jit(solution)/shard_map/slice | solution.py:100
  75.8 4.4 %all-to-all-start.1 = ((bf16[8,1,64,512]{3,2,1,0:T(8,128)(2,1)}), bf16[8,1,64,512]{3,2,1,0:T(8,128)(2,1)}, u32[]{:S(2)}, u32[]{:S(2)}) async-start(bf16[8,1,64,512]{3,2,1,0:T(8,128)(2,1)} %bitcast.18), calls=%async_computation.1 | async-start | bytes 1048576 | tf_op jit(solution)/shard_map/all_to_all | solution.py:105
  80.2 6.9 %fusion.21 = bf16[4,128,4,128]{1,3,0,2:T(8,128)(2,1)} fusion(bf16[1536,4,128,1]{0,2,3,1:T(8,128)(2,1)} %bitcast.95, f32[4,4,128,1536]{2,3,0,1:T(8,128)} %get-tuple-element.22, f32[4,4,128]{2,0,1:T(4,128)S(1)} %get-tuple-element.21), kind=kOutput, calls=%fused_computation.33 | convolution fusion | flops 811859968 | bytes 14688256 | tf_op jit(solution)/shard_map/jhqk,khd->jqhd/dot_general | solution.py:74
  87.2 2.2 %copy.41 = bf16[4,128,4,128]{3,2,1,0:T(4,128)(2,1)} copy(bf16[4,128,4,128]{1,3,0,2:T(8,128)(2,1)} %fusion.21) | data formatting | bytes 1048576 | tf_op jit(solution)/shard_map/convert_element_type | solution.py:75
  89.3 3.7 %scatter_custom_fusion = bf16[512,512]{1,0:T(8,128)(2,1)} fusion(s32[512]{0:T(512)S(1)} %compare_select_fusion, bf16[64,8,4,128]{3,2,1,0:T(4,128)(2,1)} %bitcast.94, bf16[]{:T(256)} %constant.71.clone.1), kind=kCustom, calls=%fused_computation.46 | custom fusion | bytes 1048578 | tf_op jit(solution)/shard_map/scatter | solution.py:76
  93.0 1.5 %all-to-all-done.1 = bf16[8,1,64,512]{3,2,1,0:T(8,128)(2,1)} async-done(((bf16[8,1,64,512]{3,2,1,0:T(8,128)(2,1)}), bf16[8,1,64,512]{3,2,1,0:T(8,128)(2,1)}, u32[]{:S(2)}, u32[]{:S(2)}) %all-to-all-start.1) | async-done | bytes 524320 | tf_op jit(solution)/shard_map/all_to_all | solution.py:105
  94.5 3.4 %fusion.15 = bf16[1,512,1024]{2,1,0:T(8,128)(2,1)} fusion(bf16[1024,1024]{1,0:T(8,128)(2,1)S(1)} %copy-done, bf16[1,512,1024]{2,1,0:T(8,128)(2,1)S(1)} %copy-done.3, bf16[512,512]{1,0:T(8,128)(2,1)} %bitcast.19, bf16[512,512]{1,0:T(8,128)(2,1)} %scatter_custom_fusion, f32[1024]{0:T(1024)S(1)} %bitcast.98), kind=kOutput, calls=%fused_computation.26 | convolution fusion | flops 1077936128 | bytes 5246976 | tf_op jit(solution)/shard_map/dot_general | solution.py:109
  (46 shorter events, 8.6 us)
Async XLA Ops:
  0.0 94.5 %copy-start = (bf16[1024,1024]{1,0:T(8,128)(2,1)S(1)}, bf16[1024,1024]{1,0:T(8,128)(2,1)}, u32[]{:S(2)}) copy-start(bf16[1024,1024]{1,0:T(8,128)(2,1)} %param.10) | copy-start | bytes 6291460
  0.0 4.7 %copy-start.2 = (bf16[1,512,1024]{2,1,0:T(8,128)(2,1)S(1)}, bf16[1,512,1024]{2,1,0:T(8,128)(2,1)}, u32[]{:S(2)}) copy-start(bf16[1,512,1024]{2,1,0:T(8,128)(2,1)} %param.7) | copy-start | bytes 3145732
  0.0 4.7 %copy-start.8 = (f32[3,1024]{1,0:T(4,128)S(1)}, f32[3,1024]{1,0:T(4,128)}, u32[]{:S(2)}) copy-start(f32[3,1024]{1,0:T(4,128)} %param.8) | copy-start | bytes 36868
  15.8 4.9 %copy-start.4 = (bf16[512,512]{1,0:T(8,128)(2,1)S(1)}, bf16[512,512]{1,0:T(8,128)(2,1)}, u32[]{:S(2)}) copy-start(bf16[512,512]{1,0:T(8,128)(2,1)} %get-tuple-element.6) | copy-start | bytes 1572868
  15.8 4.9 %copy-start.5 = (bf16[512,512]{1,0:T(8,128)(2,1)S(1)}, bf16[512,512]{1,0:T(8,128)(2,1)}, u32[]{:S(2)}) copy-start(bf16[512,512]{1,0:T(8,128)(2,1)} %get-tuple-element.7) | copy-start | bytes 1572868
  15.8 4.9 %copy-start.6 = (bf16[512,512]{1,0:T(8,128)(2,1)S(1)}, bf16[512,512]{1,0:T(8,128)(2,1)}, u32[]{:S(2)}) copy-start(bf16[512,512]{1,0:T(8,128)(2,1)} %get-tuple-element.8) | copy-start | bytes 1572868
  18.3 26.2 %collective-permute-start.1 = (bf16[512,1024]{1,0:T(8,128)(2,1)}, bf16[512,1024]{1,0:T(8,128)(2,1)}, u32[]{:S(2)}, u32[]{:S(2)}) collective-permute-start(bf16[512,1024]{1,0:T(8,128)(2,1)} %broadcast_select_fusion), channel_id=1, source_target_pairs={{8,0},{16,8},{24,16},{0,24},{9,1},{17,9},{25,17},{1,25},{10,2},{18... | collective-permute-start | bytes 3145736 | tf_op jit(solution)/shard_map/ppermute | solution.py:19
  20.6 24.9 %collective-permute-start = (bf16[512,1024]{1,0:T(8,128)(2,1)}, bf16[512,1024]{1,0:T(8,128)(2,1)}, u32[]{:S(2)}, u32[]{:S(2)}) collective-permute-start(bf16[512,1024]{1,0:T(8,128)(2,1)} %broadcast_select_fusion), channel_id=1, source_target_pairs={{0,8},{8,16},{16,24},{24,0},{1,9},{9,17},{17,25},{25,1},{2,10},{10... | collective-permute-start | bytes 3145736 | tf_op jit(solution)/shard_map/ppermute | solution.py:17
  21.9 6.0 %copy-start.9 = (s32[4,4]{1,0:T(4,128)S(1)}, s32[4,4]{1,0:T(4,128)}, u32[]{:S(2)}) copy-start(s32[4,4]{1,0:T(4,128)} %param.12) | copy-start | bytes 196
  21.9 6.0 %copy-start.10 = (s32[4]{0:T(128)S(1)}, s32[4]{0:T(128)}, u32[]{:S(2)}) copy-start(s32[4]{0:T(128)} %param.13) | copy-start | bytes 52
  21.9 6.3 %copy-start.1 = (bf16[512,512]{1,0:T(8,128)(2,1)S(1)}, bf16[512,512]{1,0:T(8,128)(2,1)}, u32[]{:S(2)}) copy-start(bf16[512,512]{1,0:T(8,128)(2,1)} %get-tuple-element.5) | copy-start | bytes 1572868
  21.9 43.9 %all-to-all-start = ((bf16[1,8,64,1536]{3,2,0,1:T(8,128)(2,1)}), bf16[1,8,64,1536]{3,2,0,1:T(8,128)(2,1)}, u32[]{:S(2)}, u32[]{:S(2)}) async-start(bf16[1,8,64,1536]{3,2,0,1:T(8,128)(2,1)} %bitcast.93), calls=%async_computation | async-start | bytes 3145728 | tf_op jit(solution)/shard_map/all_to_all | solution.py:84
  28.2 2.2 %copy-start.7 = (s32[512]{0:T(512)S(1)}, s32[512]{0:T(512)}, u32[]{:S(2)}) copy-start(s32[512]{0:T(512)} %param.11) | copy-start | bytes 6148
  75.8 18.7 %all-to-all-start.1 = ((bf16[8,1,64,512]{3,2,1,0:T(8,128)(2,1)}), bf16[8,1,64,512]{3,2,1,0:T(8,128)(2,1)}, u32[]{:S(2)}, u32[]{:S(2)}) async-start(bf16[8,1,64,512]{3,2,1,0:T(8,128)(2,1)} %bitcast.18), calls=%async_computation.1 | async-start | bytes 1048576 | tf_op jit(solution)/shard_map/all_to_all | solution.py:105
  87.2 7.4 %copy-start.3 = (bf16[1,512,1024]{2,1,0:T(8,128)(2,1)S(1)}, bf16[1,512,1024]{2,1,0:T(8,128)(2,1)}, u32[]{:S(2)}) copy-start(bf16[1,512,1024]{2,1,0:T(8,128)(2,1)} %param.7) | copy-start | bytes 3145732
where the time goes:
time: 98.6 us; the launch traced here: 97.9 us
  matrix products  28.7 us (29%)
  local copies, waits for them, and re-layouts  26.5 us (27%)
  waiting for transfers between devices  18.5 us (19%)
  starting transfers between devices  12.7 us (13%)
  other arithmetic  11.3 us (11%)
    ppermute x1, waiting for transfers between devices, with_halo(): lax.ppermute(head, axis, [((i + 1) % count, i) for i in range(count)])  14.1 us
    sub x1, matrix products, softmax_last(): expo = jnp.exp(scores - top)  9.29 us
    dot_general x1, matrix products, body(): jnp.einsum('jhqk,khd->jqhd', weights, vals, preferred_element_type=jnp.fl...  6.91 us
    dot_general x1, matrix products, body(): jnp.dot(modulated, w_qkv, preferred_element_type=jnp.float32)  6.71 us
    all_to_all x1, starting transfers between devices, body(): lax.all_to_all(stacked, 'frame', split_axis=1, concat_axis=0, tiled=True)  5.97 us
    slice x2, local copies, waits for them, and re-layouts, body(): keys = window[:, :half].reshape(3 * tokens, sheads, head_dim)  4.49 us
    all_to_all x1, starting transfers between devices, body(): lax.all_to_all(mixed_frames, 'frame', split_axis=0, concat_axis=1, tiled=...  4.39 us
    reshape x1, local copies, waits for them, and re-layouts, body(): parts = group.reshape(frame_count, count, 3, sheads, head_dim)  3.96 us
  transfers between devices with their start and end apart: 4, of which 4 were waited for; matrix products, arithmetic and copies ran while one was open for 36% of the time, Pallas kernels for 0%

commit v1 on v0

v1 whole, which is shorter than its diff:
```python
import functools

import jax
import jax.numpy as jnp
from jax import lax
from jax.experimental import pallas as pl
from jax.experimental.pallas import tpu as pltpu
from jax.sharding import PartitionSpec as P

HEADS = 8
MAXNB = 4
MESH = pl.DeviceIdType.MESH
F32 = jnp.float32
BF16 = jnp.bfloat16
CHUNK = 16


def modulate(rows, cond_ref):
    rows = rows.astype(F32)
    centred = rows - jnp.mean(rows, axis=-1, keepdims=True)
    normed = centred * lax.rsqrt(jnp.mean(centred * centred, axis=-1, keepdims=True) + 1e-06)
    return (normed * (1.0 + cond_ref[1:2, :]) + cond_ref[0:1, :]).astype(BF16)


def dot(a, b):
    return jnp.dot(a, b, preferred_element_type=F32)


def dot_t(a, b):
    return lax.dot_general(a, b, (((1,), (1,)), ((), ())), preferred_element_type=F32)


def kernel(
    clip,
    lat_hbm,
    cond_ref,
    wqkv_hbm,
    wout_hbm,
    slot_ref,
    nb_ref,
    cnt_ref,
    out_hbm,
    lat,
    wqkv,
    wout,
    grp,
    mod,
    ranked,
    query,
    kwin,
    vwin,
    place,
    block_out,
    sp_mixed,
    t_out,
    tmp,
    out_v,
    local_sem,
    own_sem,
    lat_send,
    lat_recv,
    halo_send,
    halo_recv,
    ret_send,
    ret_recv,
    out_sem,
):
    space_total = lax.axis_size("space")
    me_s = lax.axis_index("space")
    me_f = lax.axis_index("frame")
    rank = lax.rem(me_f, clip)
    base = me_f - rank
    left = lax.rem(me_s + space_total - 1, space_total)
    right = lax.rem(me_s + 1, space_total)
    per, width = lat.shape[1], lat.shape[2]
    tokens = clip * per
    half = width // 2
    head_dim = width // HEADS
    sheads = HEADS // 2
    blocks, block_len = slot_ref.shape
    chunks = per // CHUNK
    rows = clip * CHUNK
    scale = 1.0 / (head_dim**0.5)

    def peer_of(p):
        return lax.rem(rank + p, clip)

    lat_in = pltpu.make_async_copy(lat_hbm, lat, local_sem.at[0])
    wqkv_in = pltpu.make_async_copy(wqkv_hbm, wqkv, local_sem.at[1])
    wout_in = pltpu.make_async_copy(wout_hbm, wout, local_sem.at[2])

    def own_copy(c):
        return pltpu.make_async_copy(
            lat_hbm.at[rank, pl.ds(pl.multiple_of(c * CHUNK, CHUNK), CHUNK)],
            grp.at[c, rank],
            own_sem.at[c],
        )

    def lat_copy(c, peer, slot):
        return pltpu.make_async_remote_copy(
            src_ref=lat_hbm.at[peer, pl.ds(pl.multiple_of(c * CHUNK, CHUNK), CHUNK)],
            dst_ref=grp.at[c, slot],
            send_sem=lat_send.at[c, peer],
            recv_sem=lat_recv.at[c, slot],
            device_id={"frame": base + peer},
            device_id_type=MESH,
        )

    def ret_copy(c, peer, slot):
        return pltpu.make_async_remote_copy(
            src_ref=t_out.at[c, peer],
            dst_ref=tmp.at[c, slot],
            send_sem=ret_send.at[c, peer],
            recv_sem=ret_recv.at[c, slot],
            device_id={"frame": base + peer},
            device_id_type=MESH,
        )

    def halo_copy(win, kind, side):
        return pltpu.make_async_remote_copy(
            src_ref=win.at[pl.ds(blocks, blocks)],
            dst_ref=win.at[pl.ds(2 * blocks * side, blocks)],
            send_sem=halo_send.at[kind, side],
            recv_sem=halo_recv.at[kind, side],
            device_id={"space": left if side else right},
            device_id_type=MESH,
        )

    def out_copy(c):
        cut = pl.ds(pl.multiple_of(c * CHUNK, CHUNK), CHUNK)
        return pltpu.make_async_copy(out_v.at[:, cut], out_hbm.at[:, cut], out_sem.at[c])

    barrier = pltpu.get_barrier_semaphore()

    @pl.loop(1, clip)
    def _(p):
        pl.semaphore_signal(
            barrier, inc=1, device_id={"frame": base + peer_of(p)}, device_id_type=MESH
        )

    for side in (left, right):
        pl.semaphore_signal(barrier, inc=1, device_id={"space": side}, device_id_type=MESH)
    lat_in.start()
    wqkv_in.start()

    @pl.loop(0, chunks)
    def _(c):
        own_copy(c).start()

    pl.semaphore_wait(barrier, clip + 1)

    @pl.loop(0, chunks)
    def _(c):
        @pl.loop(1, clip)
        def _(p):
            lat_copy(c, peer_of(p), rank).start()

    wout_in.start()
    lat_in.wait()

    @pl.loop(0, clip)
    def _(i):
        mod[pl.ds(pl.multiple_of(i * per, per), per), :] = modulate(lat[i], cond_ref)

    for b in range(blocks):
        cut = slice(b * block_len, (b + 1) * block_len)
        spots = lax.broadcasted_iota(jnp.int32, (tokens, block_len), 0)
        one_hot = jnp.where(spots == slot_ref[b : b + 1, :], 1.0, 0.0).astype(BF16)
        place[:, cut] = one_hot
        ranked[cut, :] = lax.dot_general(
            one_hot, mod[...], (((0,), (0,)), ((), ())), preferred_element_type=F32
        ).astype(BF16)

    wqkv_in.wait()
    for kind, win in enumerate((kwin, vwin)):
        for lo in range(0, half, 256):
            at = (kind + 1) * width + lo
            part = dot(ranked[...], wqkv[:, at : at + 256]).astype(BF16)
            win[blocks : 2 * blocks, :, lo : lo + 256] = part.reshape(blocks, block_len, 256)
        for side in range(2):
            halo_copy(win, kind, side).start()
    for lo in range(0, half, 256):
        part = dot(ranked[...], wqkv[:, lo : lo + 256]).astype(BF16)
        query[:, :, lo : lo + 256] = part.reshape(blocks, block_len, 256)

    same = lax.rem(lax.broadcasted_iota(jnp.int32, (rows, rows), 0), CHUNK) == lax.rem(
        lax.broadcasted_iota(jnp.int32, (rows, rows), 1), CHUNK
    )

    @pl.loop(0, chunks)
    def _(c):
        own_copy(c).wait()

        @pl.loop(1, clip)
        def _(p):
            lat_copy(c, peer_of(p), peer_of(p)).wait_recv()

        normed = modulate(grp[c].reshape(rows, width), cond_ref)
        q = dot(normed, wqkv[:, half:width]).astype(BF16)
        k = dot(normed, wqkv[:, width + half : 2 * width]).astype(BF16)
        v = dot(normed, wqkv[:, 2 * width + half :]).astype(BF16)
        outs = []
        for h in range(sheads):
            cut = slice(h * head_dim, (h + 1) * head_dim)
            scores = jnp.where(same, dot_t(q[:, cut], k[:, cut]) * scale, -jnp.inf)
            expo = jnp.exp(scores - jnp.max(scores, axis=-1, keepdims=True))
            total = jnp.sum(expo, axis=-1, keepdims=True)
            outs.append((dot(expo.astype(BF16), v[:, cut]) / total).astype(BF16))
        result = jnp.concatenate(outs, axis=1).reshape(clip, CHUNK, half)
        t_out[c] = result
        tmp[c, rank] = t_out[c, rank]

        @pl.loop(1, clip)
        def _(p):
            ret_copy(c, peer_of(p), rank).start()

    for kind, win in enumerate((kwin, vwin)):
        for side in range(2):
            halo_copy(win, kind, side).wait_recv()
    first_block = (me_s - 1) * blocks
    total_blocks = blocks * space_total

    @pl.loop(0, blocks)
    def _(b):
        ids = []
        for n in range(MAXNB):
            at = nb_ref[b, n] - first_block
            at = jnp.where(at >= total_blocks, at - total_blocks, at)
            at = jnp.where(at < 0, at + total_blocks, at)
            ids.append(jnp.clip(at, 0, 3 * blocks - 1))
        keys = [kwin[at] for at in ids]
        vals = [vwin[at] for at in ids]
        q = query[b]
        outs = []
        for h in range(sheads):
            cut = slice(h * head_dim, (h + 1) * head_dim)
            parts = []
            for n in range(MAXNB):
                part = dot_t(q[:, cut], keys[n][:, cut]) * scale
                if n > 0:
                    part = jnp.where(n < cnt_ref[b], part, -jnp.inf)
                parts.append(part)
            scores = jnp.concatenate(parts, axis=1)
            expo = jnp.exp(scores - jnp.max(scores, axis=-1, keepdims=True))
            total = jnp.sum(expo, axis=-1, keepdims=True)
            val = jnp.concatenate([vals[n][:, cut] for n in range(MAXNB)], axis=0)
            outs.append((dot(expo.astype(BF16), val) / total).astype(BF16))
        block_out[pl.ds(pl.multiple_of(b * block_len, block_len), block_len), :] = (
            jnp.concatenate(outs, axis=1)
        )

    spatial = dot(place[...], block_out[...]).astype(BF16)
    wout_in.wait()
    for lo in range(0, width, 256):
        part = dot(spatial, wout[:half, lo : lo + 256])
        sp_mixed[:, :, lo : lo + 256] = part.reshape(clip, per, 256)

    @pl.loop(0, chunks)
    def _(c):
        @pl.loop(1, clip)
        def _(p):
            ret_copy(c, peer_of(p), peer_of(p)).wait_recv()

        cut = pl.ds(pl.multiple_of(c * CHUNK, CHUNK), CHUNK)
        mixed = dot(tmp[c].reshape(rows, half), wout[half:, :]).reshape(clip, CHUNK, width)
        mixed = mixed + sp_mixed[:, cut, :]
        gate = cond_ref[2:3, :].reshape(1, 1, width)
        out_v[:, cut, :] = (lat[:, cut, :].astype(F32) + gate * mixed).astype(BF16)
        out_copy(c).start()

    @pl.loop(0, chunks)
    def _(c):
        out_copy(c).wait()

        @pl.loop(1, clip)
        def _(p):
            lat_copy(c, peer_of(p), rank).wait_send()
            ret_copy(c, peer_of(p), rank).wait_send()

    for kind, win in enumerate((kwin, vwin)):
        for side in range(2):
            halo_copy(win, kind, side).wait_send()


def body(latent, cond, w_qkv, w_out, slot, neighbours, counts):
    tokens, width = latent.shape[1], latent.shape[2]
    blocks = neighbours.shape[0]
    block_len = tokens // blocks
    half = width // 2
    clip = min(8, lax.axis_size("frame"))
    per = tokens // clip
    chunks = per // CHUNK
    vmem = pl.BlockSpec(memory_space=pltpu.VMEM)
    smem = pl.BlockSpec(memory_space=pltpu.SMEM)
    hbm = pl.BlockSpec(memory_space=pl.ANY)
    dma = pltpu.SemaphoreType.DMA
    out = pl.pallas_call(
        functools.partial(kernel, clip),
        out_shape=jax.ShapeDtypeStruct((clip, per, width), BF16),
        in_specs=[hbm, vmem, hbm, hbm, vmem, smem, smem],
        out_specs=hbm,
        scratch_shapes=[
            pltpu.VMEM((clip, per, width), BF16),
            pltpu.VMEM(w_qkv.shape, BF16),
            pltpu.VMEM(w_out.shape, BF16),
            pltpu.VMEM((chunks, clip, CHUNK, width), BF16),
            pltpu.VMEM((tokens, width), BF16),
            pltpu.VMEM((tokens, width), BF16),
            pltpu.VMEM((blocks, block_len, half), BF16),
            pltpu.VMEM((3 * blocks, block_len, half), BF16),
            pltpu.VMEM((3 * blocks, block_len, half), BF16),
            pltpu.VMEM((tokens, tokens), BF16),
            pltpu.VMEM((tokens, half), BF16),
            pltpu.VMEM((clip, per, width), F32),
            pltpu.VMEM((chunks, clip, CHUNK, half), BF16),
            pltpu.VMEM((chunks, clip, CHUNK, half), BF16),
            pltpu.VMEM((clip, per, width), BF16),
            dma((3,)),
            dma((chunks,)),
            dma((chunks, clip)),
            dma((chunks, clip)),
            dma((2, 2)),
            dma((2, 2)),
            dma((chunks, clip)),
            dma((chunks, clip)),
            dma((chunks,)),
        ],
        compiler_params=pltpu.CompilerParams(
            collective_id=0, has_side_effects=True, vmem_limit_bytes=48 * 1024 * 1024
        ),
        cost_estimate=pl.CostEstimate(
            flops=5_000_000_000, bytes_accessed=12_000_000, transcendentals=2_000_000
        ),
    )(
        latent.reshape(clip, per, width),
        cond,
        w_qkv,
        w_out,
        slot.reshape(blocks, block_len),
        neighbours,
        counts,
    )
    return out.reshape(1, tokens, width)


def solution(mesh):
    in_specs = (P("frame", "space", None), P(), P(), P(), P("space"), P("space", None), P("space"))
    out_specs = P("frame", "space", None)
    return jax.shard_map(body, mesh=mesh, in_specs=in_specs, out_specs=out_specs, check_vma=False)
```

time: 98.6 us -> 51.6 us (0.52)
  Pallas kernels: 0 us -> 44.6 us
  matrix products: 28.7 us -> 0 us
  local copies, waits for them, and re-layouts: 26.5 us -> 6.52 us
  waiting for transfers between devices: 18.5 us -> 0 us
  starting transfers between devices: 12.7 us -> 0 us
  other arithmetic: 11.3 us -> 0 us
    pallas_call x0 -> x1, Pallas kernels: none -> 44.6 us  [body(): pl.pallas_call(functools.partial(kernel, clip), out_shape=jax.ShapeDtypeS...]
    dot_general x5 -> x0, matrix products: 19.4 us -> none  [the longest x1 6.91 us: body(): jnp.einsum('jhqk,khd->jqhd', weights, vals, preferred_element_type=jnp.fl...]
    ppermute x2 -> x0, waiting for transfers between devices: 15.1 us -> none  [the longest x1 14.1 us: with_halo(): lax.ppermute(head, axis, [((i + 1) % count, i) for i in range(count)])]
    slice x5 -> x0, local copies, waits for them, and re-layouts: 10.5 us -> none  [the longest x2 4.49 us: body(): keys = window[:, :half].reshape(3 * tokens, sheads, head_dim)]
    all_to_all x2 -> x0, starting transfers between devices: 10.4 us -> none  [the longest x1 5.97 us: body(): lax.all_to_all(stacked, 'frame', split_axis=1, concat_axis=0, tiled=True)]
    sub x1 -> x0, matrix products: 9.29 us -> none  [softmax_last(): expo = jnp.exp(scores - top)]
    unnamed x24 -> x13, local copies, waits for them, and re-layouts: 0.13 us -> 6.52 us
    reshape x2 -> x0, local copies, waits for them, and re-layouts: 4.95 us -> none  [the longest x1 3.96 us: body(): parts = group.reshape(frame_count, count, 3, sheads, head_dim)]
  transfers between devices with their start and end apart: 4 -> 0, of which waited for: 4 -> 0; matrix products, arithmetic and copies ran while one was open for 36% -> 0% of each run, Pallas kernels for 0% -> 0%
where the time goes in v1:
time: 51.6 us; the launch traced here: 51.1 us
  Pallas kernels  44.6 us (86%)
  local copies, waits for them, and re-layouts  6.52 us (13%)
    pallas_call x1, Pallas kernels, body(): pl.pallas_call(functools.partial(kernel, clip), out_shape=jax.ShapeDtypeS...  44.6 us
    unnamed x13, local copies, waits for them, and re-layouts  6.52 us

profile of v1, /device:TPU:0, one launch (start us, length us, event | category | flops | bytes accessed | tf_op | source)
XLA Modules:
  0.0 51.1 jit_solution(11109826129741573878)
XLA Ops:
  0.0 0.0 copy-start
  0.0 1.6 %copy-done = bf16[1024,1024]{1,0:T(8,128)(2,1)S(1)} copy-done((bf16[1024,1024]{1,0:T(8,128)(2,1)S(1)}, bf16[1024,1024]{1,0:T(8,128)(2,1)}, u32[]{:S(2)}) %copy-start) | copy-done | bytes 2097176
  1.6 0.0 copy-start.1
  1.6 1.2 %copy-done.1 = bf16[1,512,1024]{2,1,0:T(8,128)(2,1)S(1)} copy-done((bf16[1,512,1024]{2,1,0:T(8,128)(2,1)S(1)}, bf16[1,512,1024]{2,1,0:T(8,128)(2,1)}, u32[]{:S(2)}) %copy-start.1) | copy-done | bytes 1048600
  2.8 0.0 copy-start.2
  2.8 0.7 %copy-done.2 = f32[3,1024]{1,0:T(4,128)S(1)} copy-done((f32[3,1024]{1,0:T(4,128)S(1)}, f32[3,1024]{1,0:T(4,128)}, u32[]{:S(2)}) %copy-start.2) | copy-done | bytes 12312
  3.5 0.0 copy-start.3
  3.5 0.7 %copy-done.3 = s32[512]{0:T(512)S(1)} copy-done((s32[512]{0:T(512)S(1)}, s32[512]{0:T(512)}, u32[]{:S(2)}) %copy-start.3) | copy-done | bytes 2072
  4.2 0.0 copy-start.4
  4.2 0.7 %copy-done.4 = s32[4,4]{1,0:T(4,128)S(1)} copy-done((s32[4,4]{1,0:T(4,128)S(1)}, s32[4,4]{1,0:T(4,128)}, u32[]{:S(2)}) %copy-start.4) | copy-done | bytes 88
  4.9 0.0 copy-start.5
  4.9 0.7 %copy-done.5 = s32[4]{0:T(128)S(1)} copy-done((s32[4]{0:T(128)S(1)}, s32[4]{0:T(128)}, u32[]{:S(2)}) %copy-start.5) | copy-done | bytes 40
  5.6 44.6 %shard_map.73 = bf16[8,64,1024]{2,1,0:T(8,128)(2,1)S(1)} custom-call(bf16[8,64,1024]{2,1,0:T(8,128)(2,1)S(1)} %bitcast.4, f32[3,1024]{1,0:T(4,128)S(1)} %copy-done.2, bf16[1024,3072]{1,0:T(8,128)(2,1)} %wqkv_hbm.1, bf16[1024,1024]{1,0:T(8,128)(2,1)S(1)} %copy-done, s32[4,128]{1,0:T(4,128)S(1)} %bitcast.5, s32[4,4]{1,0:T(4,128)S(1)} %copy-done.4, s32[4]{0:T(128)S(1)} %copy-done.5), custom_call_target="tpu_custom_call" | custom-call | flops 5000000000 | bytes 12000000 | tf_op jit(solution)/shard_map/pallas_call | solution.py:297
  50.2 1.0 %copy.9 = bf16[1,512,1024]{2,1,0:T(8,128)(2,1)} copy(bf16[1,512,1024]{2,1,0:T(8,128)(2,1)S(1)} %bitcast.3) | data formatting | bytes 2097152
Async XLA Ops:
  0.0 1.6 %copy-start = (bf16[1024,1024]{1,0:T(8,128)(2,1)S(1)}, bf16[1024,1024]{1,0:T(8,128)(2,1)}, u32[]{:S(2)}) copy-start(bf16[1024,1024]{1,0:T(8,128)(2,1)} %wout_hbm.1) | copy-start | bytes 6291460
  1.6 1.2 %copy-start.1 = (bf16[1,512,1024]{2,1,0:T(8,128)(2,1)S(1)}, bf16[1,512,1024]{2,1,0:T(8,128)(2,1)}, u32[]{:S(2)}) copy-start(bf16[1,512,1024]{2,1,0:T(8,128)(2,1)} %param.7) | copy-start | bytes 3145732
  2.8 0.7 %copy-start.2 = (f32[3,1024]{1,0:T(4,128)S(1)}, f32[3,1024]{1,0:T(4,128)}, u32[]{:S(2)}) copy-start(f32[3,1024]{1,0:T(4,128)} %cond_ref.1) | copy-start | bytes 36868
  3.5 0.7 %copy-start.3 = (s32[512]{0:T(512)S(1)}, s32[512]{0:T(512)}, u32[]{:S(2)}) copy-start(s32[512]{0:T(512)} %param.11) | copy-start | bytes 6148
  4.2 0.7 %copy-start.4 = (s32[4,4]{1,0:T(4,128)S(1)}, s32[4,4]{1,0:T(4,128)}, u32[]{:S(2)}) copy-start(s32[4,4]{1,0:T(4,128)} %nb_ref.1) | copy-start | bytes 196
  4.9 0.7 %copy-start.5 = (s32[4]{0:T(128)S(1)}, s32[4]{0:T(128)}, u32[]{:S(2)}) copy-start(s32[4]{0:T(128)} %cnt_ref.1) | copy-start | bytes 52

commit v2 on v1

--- a/solution.py
+++ b/solution.py
@@ -1,4 +1,5 @@
 import functools
+import math
 
 import jax
 import jax.numpy as jnp
@@ -33,13 +34,17 @@
 def kernel(
     clip,
     lat_hbm,
-    cond_ref,
+    cond_hbm,
     wqkv_hbm,
     wout_hbm,
+    slot_hbm,
+    nb_hbm,
+    cnt_hbm,
+    out_hbm,
+    cond_ref,
     slot_ref,
     nb_ref,
     cnt_ref,
-    out_hbm,
     lat,
     wqkv,
     wout,
@@ -80,7 +85,9 @@
     blocks, block_len = slot_ref.shape
     chunks = per // CHUNK
     rows = clip * CHUNK
-    scale = 1.0 / (head_dim**0.5)
+    scale = math.log2(math.e) / math.sqrt(head_dim)
+
+    far_first = sorted(range(1, clip), key=lambda p: abs(2 * p - clip))
 
     def peer_of(p):
         return lax.rem(rank + p, clip)
@@ -88,6 +95,12 @@
     lat_in = pltpu.make_async_copy(lat_hbm, lat, local_sem.at[0])
     wqkv_in = pltpu.make_async_copy(wqkv_hbm, wqkv, local_sem.at[1])
     wout_in = pltpu.make_async_copy(wout_hbm, wout, local_sem.at[2])
+    small_in = [
+        pltpu.make_async_copy(cond_hbm, cond_ref, local_sem.at[3]),
+        pltpu.make_async_copy(slot_hbm, slot_ref, local_sem.at[4]),
+        pltpu.make_async_copy(nb_hbm, nb_ref, local_sem.at[5]),
+        pltpu.make_async_copy(cnt_hbm, cnt_ref, local_sem.at[6]),
+    ]
 
     def own_copy(c):
         return pltpu.make_async_copy(
@@ -141,6 +154,8 @@
     for side in (left, right):
         pl.semaphore_signal(barrier, inc=1, device_id={"space": side}, device_id_type=MESH)
     lat_in.start()
+    for copy in small_in:
+        copy.start()
     wqkv_in.start()
 
     @pl.loop(0, chunks)
@@ -151,11 +166,12 @@
 
     @pl.loop(0, chunks)
     def _(c):
-        @pl.loop(1, clip)
-        def _(p):
+        for p in far_first:
             lat_copy(c, peer_of(p), rank).start()
 
     wout_in.start()
+    for copy in small_in:
+        copy.wait()
     lat_in.wait()
 
     @pl.loop(0, clip)
@@ -202,16 +218,15 @@
         outs = []
         for h in range(sheads):
             cut = slice(h * head_dim, (h + 1) * head_dim)
-            scores = jnp.where(same, dot_t(q[:, cut], k[:, cut]) * scale, -jnp.inf)
-            expo = jnp.exp(scores - jnp.max(scores, axis=-1, keepdims=True))
+            scores = jnp.where(same, dot_t(q[:, cut], k[:, cut]), -jnp.inf)
+            expo = jnp.exp2((scores - jnp.max(scores, axis=-1, keepdims=True)) * scale)
             total = jnp.sum(expo, axis=-1, keepdims=True)
             outs.append((dot(expo.astype(BF16), v[:, cut]) / total).astype(BF16))
         result = jnp.concatenate(outs, axis=1).reshape(clip, CHUNK, half)
         t_out[c] = result
         tmp[c, rank] = t_out[c, rank]
 
-        @pl.loop(1, clip)
-        def _(p):
+        for p in far_first:
             ret_copy(c, peer_of(p), rank).start()
 
     for kind, win in enumerate((kwin, vwin)):
@@ -236,12 +251,12 @@
             cut = slice(h * head_dim, (h + 1) * head_dim)
             parts = []
             for n in range(MAXNB):
-                part = dot_t(q[:, cut], keys[n][:, cut]) * scale
+                part = dot_t(q[:, cut], keys[n][:, cut])
                 if n > 0:
                     part = jnp.where(n < cnt_ref[b], part, -jnp.inf)
                 parts.append(part)
             scores = jnp.concatenate(parts, axis=1)
-            expo = jnp.exp(scores - jnp.max(scores, axis=-1, keepdims=True))
+            expo = jnp.exp2((scores - jnp.max(scores, axis=-1, keepdims=True)) * scale)
             total = jnp.sum(expo, axis=-1, keepdims=True)
             val = jnp.concatenate([vals[n][:, cut] for n in range(MAXNB)], axis=0)
             outs.append((dot(expo.astype(BF16), val) / total).astype(BF16))
@@ -290,16 +305,18 @@
     clip = min(8, lax.axis_size("frame"))
     per = tokens // clip
     chunks = per // CHUNK
-    vmem = pl.BlockSpec(memory_space=pltpu.VMEM)
-    smem = pl.BlockSpec(memory_space=pltpu.SMEM)
-    hbm = pl.BlockSpec(memory_space=pl.ANY)
+    hbm = pl.BlockSpec(memory_space=pltpu.HBM)
     dma = pltpu.SemaphoreType.DMA
     out = pl.pallas_call(
         functools.partial(kernel, clip),
         out_shape=jax.ShapeDtypeStruct((clip, per, width), BF16),
-        in_specs=[hbm, vmem, hbm, hbm, vmem, smem, smem],
+        in_specs=[hbm] * 7,
         out_specs=hbm,
         scratch_shapes=[
+            pltpu.VMEM(cond.shape, F32),
+            pltpu.VMEM((blocks, block_len), jnp.int32),
+            pltpu.SMEM(neighbours.shape, jnp.int32),
+            pltpu.SMEM(counts.shape, jnp.int32),
             pltpu.VMEM((clip, per, width), BF16),
             pltpu.VMEM(w_qkv.shape, BF16),
             pltpu.VMEM(w_out.shape, BF16),
@@ -315,7 +332,7 @@
             pltpu.VMEM((chunks, clip, CHUNK, half), BF16),
             pltpu.VMEM((chunks, clip, CHUNK, half), BF16),
             pltpu.VMEM((clip, per, width), BF16),
-            dma((3,)),
+            dma((7,)),
             dma((chunks,)),
             dma((chunks, clip)),
             dma((chunks, clip)),
@@ -332,13 +349,18 @@
             flops=5_000_000_000, bytes_accessed=12_000_000, transcendentals=2_000_000
         ),
     )(
-        latent.reshape(clip, per, width),
-        cond,
-        w_qkv,
-        w_out,
-        slot.reshape(blocks, block_len),
-        neighbours,
-        counts,
+        *(
+            pltpu.with_memory_space_constraint(x, pltpu.HBM)
+            for x in (
+                latent.reshape(clip, per, width),
+                cond,
+                w_qkv,
+                w_out,
+                slot.reshape(blocks, block_len),
+                neighbours,
+                counts,
+            )
+        )
     )
     return out.reshape(1, tokens, width)
 

time: 51.6 us -> 45.5 us (0.88)
  local copies, waits for them, and re-layouts: 6.52 us -> 0.97 us
    unnamed x13 -> x1, local copies, waits for them, and re-layouts: 6.52 us -> 0.97 us
where the time goes in v2:
time: 45.5 us; the launch traced here: 45.3 us
  Pallas kernels  44.4 us (98%)
  local copies, waits for them, and re-layouts  0.97 us (2%)
    pallas_call x1, Pallas kernels, body(): pl.pallas_call(functools.partial(kernel, clip), out_shape=jax.ShapeDtypeS...  44.4 us
    unnamed x1, local copies, waits for them, and re-layouts  0.97 us

profile of v2, /device:TPU:0, one launch (start us, length us, event | category | flops | bytes accessed | tf_op | source)
XLA Modules:
  0.0 45.3 jit_solution(3188478809533584868)
XLA Ops:
  0.0 44.4 %shard_map.73 = bf16[8,64,1024]{2,1,0:T(8,128)(2,1)S(1)} custom-call(bf16[8,64,1024]{2,1,0:T(8,128)(2,1)} %bitcast.4, f32[3,1024]{1,0:T(4,128)} %cond_hbm.1, bf16[1024,3072]{1,0:T(8,128)(2,1)} %wqkv_hbm.1, bf16[1024,1024]{1,0:T(8,128)(2,1)} %wout_hbm.1, s32[4,128]{1,0:T(4,128)} %bitcast.5, s32[4,4]{1,0:T(4,128)} %nb_hbm.1, s32[4]{0:T(128)} %cnt_hbm.1), custom_call_target="tpu_custom_call" | custom-call | flops 5000000000 | bytes 12000000 | tf_op jit(solution)/shard_map/pallas_call | solution.py:310
  44.4 1.0 %copy.9 = bf16[1,512,1024]{2,1,0:T(8,128)(2,1)} copy(bf16[1,512,1024]{2,1,0:T(8,128)(2,1)S(1)} %bitcast.3) | data formatting | bytes 2097152

commit v3 on v2

--- a/solution.py
+++ b/solution.py
@@ -129,12 +129,13 @@
             device_id_type=MESH,
         )
 
-    def halo_copy(win, kind, side):
+    def halo_copy(win, kind, part, side):
+        at = part * (blocks // 2)
         return pltpu.make_async_remote_copy(
-            src_ref=win.at[pl.ds(blocks, blocks)],
-            dst_ref=win.at[pl.ds(2 * blocks * side, blocks)],
-            send_sem=halo_send.at[kind, side],
-            recv_sem=halo_recv.at[kind, side],
+            src_ref=win.at[pl.ds(blocks + at, blocks // 2)],
+            dst_ref=win.at[pl.ds(2 * blocks * side + at, blocks // 2)],
+            send_sem=halo_send.at[kind, part, side],
+            recv_sem=halo_recv.at[kind, part, side],
             device_id={"space": left if side else right},
             device_id_type=MESH,
         )
@@ -164,10 +165,11 @@
 
     pl.semaphore_wait(barrier, clip + 1)
 
-    @pl.loop(0, chunks)
-    def _(c):
+    def send_latent(c):
         for p in far_first:
             lat_copy(c, peer_of(p), rank).start()
+
+    send_latent(0)
 
     wout_in.start()
     for copy in small_in:
@@ -193,8 +195,14 @@
             at = (kind + 1) * width + lo
             part = dot(ranked[...], wqkv[:, at : at + 256]).astype(BF16)
             win[blocks : 2 * blocks, :, lo : lo + 256] = part.reshape(blocks, block_len, 256)
-        for side in range(2):
-            halo_copy(win, kind, side).start()
+        for part in range(2):
+            for side in range(2):
+                halo_copy(win, kind, part, side).start()
+            step = 2 * kind + part + 1
+            if step < chunks:
+                send_latent(step)
+    for c in range(5, chunks):
+        send_latent(c)
     for lo in range(0, half, 256):
         part = dot(ranked[...], wqkv[:, lo : lo + 256]).astype(BF16)
         query[:, :, lo : lo + 256] = part.reshape(blocks, block_len, 256)
@@ -230,8 +238,9 @@
             ret_copy(c, peer_of(p), rank).start()
 
     for kind, win in enumerate((kwin, vwin)):
-        for side in range(2):
-            halo_copy(win, kind, side).wait_recv()
+        for part in range(2):
+            for side in range(2):
+                halo_copy(win, kind, part, side).wait_recv()
     first_block = (me_s - 1) * blocks
     total_blocks = blocks * space_total
 
@@ -293,8 +302,9 @@
             ret_copy(c, peer_of(p), rank).wait_send()
 
     for kind, win in enumerate((kwin, vwin)):
-        for side in range(2):
-            halo_copy(win, kind, side).wait_send()
+        for part in range(2):
+            for side in range(2):
+                halo_copy(win, kind, part, side).wait_send()
 
 
 def body(latent, cond, w_qkv, w_out, slot, neighbours, counts):
@@ -336,8 +346,8 @@
             dma((chunks,)),
             dma((chunks, clip)),
             dma((chunks, clip)),
-            dma((2, 2)),
-            dma((2, 2)),
+            dma((2, 2, 2)),
+            dma((2, 2, 2)),
             dma((chunks, clip)),
             dma((chunks, clip)),
             dma((chunks,)),

time: 45.5 us -> 45.6 us (level)
  no operation moved by 1% of the time
where the time goes in v3:
time: 45.6 us; the launch traced here: 45.4 us
  Pallas kernels  44.4 us (97%)
  local copies, waits for them, and re-layouts  0.97 us (2%)
    pallas_call x1, Pallas kernels, body(): pl.pallas_call(functools.partial(kernel, clip), out_shape=jax.ShapeDtypeS...  44.4 us
    unnamed x1, local copies, waits for them, and re-layouts  0.97 us

profile of v3, /device:TPU:0, one launch (start us, length us, event | category | flops | bytes accessed | tf_op | source)
XLA Modules:
  0.0 45.4 jit_solution(5823515559581034632)
XLA Ops:
  0.0 44.4 %shard_map.73 = bf16[8,64,1024]{2,1,0:T(8,128)(2,1)S(1)} custom-call(bf16[8,64,1024]{2,1,0:T(8,128)(2,1)} %bitcast.4, f32[3,1024]{1,0:T(4,128)} %cond_hbm.1, bf16[1024,3072]{1,0:T(8,128)(2,1)} %wqkv_hbm.1, bf16[1024,1024]{1,0:T(8,128)(2,1)} %wout_hbm.1, s32[4,128]{1,0:T(4,128)} %bitcast.5, s32[4,4]{1,0:T(4,128)} %nb_hbm.1, s32[4]{0:T(128)} %cnt_hbm.1), custom_call_target="tpu_custom_call" | custom-call | flops 5000000000 | bytes 12000000 | tf_op jit(solution)/shard_map/pallas_call | solution.py:320
  44.5 1.0 %copy.9 = bf16[1,512,1024]{2,1,0:T(8,128)(2,1)} copy(bf16[1,512,1024]{2,1,0:T(8,128)(2,1)S(1)} %bitcast.3) | data formatting | bytes 2097152

commit v4 on v2

--- a/solution.py
+++ b/solution.py
@@ -61,6 +61,7 @@
     tmp,
     out_v,
     local_sem,
+    w_sem,
     own_sem,
     lat_send,
     lat_recv,
@@ -93,7 +94,10 @@
         return lax.rem(rank + p, clip)
 
     lat_in = pltpu.make_async_copy(lat_hbm, lat, local_sem.at[0])
-    wqkv_in = pltpu.make_async_copy(wqkv_hbm, wqkv, local_sem.at[1])
+    w_in = []
+    for i, at in enumerate((2, 4, 0, 1, 3, 5)):
+        cut = pl.ds(at * half, half)
+        w_in.append(pltpu.make_async_copy(wqkv_hbm.at[:, cut], wqkv.at[:, cut], w_sem.at[i]))
     wout_in = pltpu.make_async_copy(wout_hbm, wout, local_sem.at[2])
     small_in = [
         pltpu.make_async_copy(cond_hbm, cond_ref, local_sem.at[3]),
@@ -129,12 +133,12 @@
             device_id_type=MESH,
         )
 
-    def halo_copy(win, kind, side):
+    def halo_copy(win, kind, b, side):
         return pltpu.make_async_remote_copy(
-            src_ref=win.at[pl.ds(blocks, blocks)],
-            dst_ref=win.at[pl.ds(2 * blocks * side, blocks)],
-            send_sem=halo_send.at[kind, side],
-            recv_sem=halo_recv.at[kind, side],
+            src_ref=win.at[blocks + b],
+            dst_ref=win.at[2 * blocks * side + b],
+            send_sem=halo_send.at[kind, side, b],
+            recv_sem=halo_recv.at[kind, side, b],
             device_id={"space": left if side else right},
             device_id_type=MESH,
         )
@@ -156,7 +160,8 @@
     lat_in.start()
     for copy in small_in:
         copy.start()
-    wqkv_in.start()
+    for copy in w_in:
+        copy.start()
 
     @pl.loop(0, chunks)
     def _(c):
@@ -164,10 +169,11 @@
 
     pl.semaphore_wait(barrier, clip + 1)
 
-    @pl.loop(0, chunks)
-    def _(c):
+    def send_latent(c):
         for p in far_first:
             lat_copy(c, peer_of(p), rank).start()
+
+    send_latent(0)
 
     wout_in.start()
     for copy in small_in:
@@ -183,28 +189,33 @@
         spots = lax.broadcasted_iota(jnp.int32, (tokens, block_len), 0)
         one_hot = jnp.where(spots == slot_ref[b : b + 1, :], 1.0, 0.0).astype(BF16)
         place[:, cut] = one_hot
-        ranked[cut, :] = lax.dot_general(
+        picked = lax.dot_general(
             one_hot, mod[...], (((0,), (0,)), ((), ())), preferred_element_type=F32
         ).astype(BF16)
-
-    wqkv_in.wait()
-    for kind, win in enumerate((kwin, vwin)):
-        for lo in range(0, half, 256):
-            at = (kind + 1) * width + lo
-            part = dot(ranked[...], wqkv[:, at : at + 256]).astype(BF16)
-            win[blocks : 2 * blocks, :, lo : lo + 256] = part.reshape(blocks, block_len, 256)
-        for side in range(2):
-            halo_copy(win, kind, side).start()
+        ranked[cut, :] = picked
+        for kind, win in enumerate((kwin, vwin)):
+            if b == 0:
+                w_in[kind].wait()
+            at = (kind + 1) * width
+            win[blocks + b] = dot(picked, wqkv[:, at : at + half]).astype(BF16)
+            for side in range(2):
+                halo_copy(win, kind, b, side).start()
+        if b + 1 < chunks:
+            send_latent(b + 1)
+    for c in range(blocks + 1, chunks):
+        send_latent(c)
+    w_in[2].wait()
     for lo in range(0, half, 256):
         part = dot(ranked[...], wqkv[:, lo : lo + 256]).astype(BF16)
         query[:, :, lo : lo + 256] = part.reshape(blocks, block_len, 256)
+    for copy in w_in[3:]:
+        copy.wait()
 
     same = lax.rem(lax.broadcasted_iota(jnp.int32, (rows, rows), 0), CHUNK) == lax.rem(
         lax.broadcasted_iota(jnp.int32, (rows, rows), 1), CHUNK
     )
 
-    @pl.loop(0, chunks)
-    def _(c):
+    def temporal(c):
         own_copy(c).wait()
 
         @pl.loop(1, clip)
@@ -229,9 +240,14 @@
         for p in far_first:
             ret_copy(c, peer_of(p), rank).start()
 
+    pl.loop(0, chunks - 1)(temporal)
+
     for kind, win in enumerate((kwin, vwin)):
         for side in range(2):
-            halo_copy(win, kind, side).wait_recv()
+
+            @pl.loop(0, blocks)
+            def _(b):
+                halo_copy(win, kind, b, side).wait_recv()
     first_block = (me_s - 1) * blocks
     total_blocks = blocks * space_total
 
@@ -264,6 +280,7 @@
             jnp.concatenate(outs, axis=1)
         )
 
+    temporal(chunks - 1)
     spatial = dot(place[...], block_out[...]).astype(BF16)
     wout_in.wait()
     for lo in range(0, width, 256):
@@ -294,7 +311,10 @@
 
     for kind, win in enumerate((kwin, vwin)):
         for side in range(2):
-            halo_copy(win, kind, side).wait_send()
+
+            @pl.loop(0, blocks)
+            def _(b):
+                halo_copy(win, kind, b, side).wait_send()
 
 
 def body(latent, cond, w_qkv, w_out, slot, neighbours, counts):
@@ -333,11 +353,12 @@
             pltpu.VMEM((chunks, clip, CHUNK, half), BF16),
             pltpu.VMEM((clip, per, width), BF16),
             dma((7,)),
+            dma((6,)),
             dma((chunks,)),
             dma((chunks, clip)),
             dma((chunks, clip)),
-            dma((2, 2)),
-            dma((2, 2)),
+            dma((2, 2, blocks)),
+            dma((2, 2, blocks)),
             dma((chunks, clip)),
             dma((chunks, clip)),
             dma((chunks,)),

time: 45.5 us -> 48.7 us (1.070)
  Pallas kernels: 44.4 us -> 47.6 us
    pallas_call x1, Pallas kernels: 44.4 us -> 47.6 us  [body(): pl.pallas_call(functools.partial(kernel, clip), out_shape=jax.ShapeDtypeS...]
where the time goes in v4:
time: 48.7 us; the launch traced here: 48.5 us
  Pallas kernels  47.6 us (98%)
  local copies, waits for them, and re-layouts  0.97 us (2%)
    pallas_call x1, Pallas kernels, body(): pl.pallas_call(functools.partial(kernel, clip), out_shape=jax.ShapeDtypeS...  47.6 us

profile of v4, /device:TPU:0, one launch (start us, length us, event | category | flops | bytes accessed | tf_op | source)
XLA Modules:
  0.0 48.5 jit_solution(16460707118297857219)
XLA Ops:
  0.0 47.6 %shard_map.73 = bf16[8,64,1024]{2,1,0:T(8,128)(2,1)S(1)} custom-call(bf16[8,64,1024]{2,1,0:T(8,128)(2,1)} %bitcast.4, f32[3,1024]{1,0:T(4,128)} %cond_hbm.1, bf16[1024,3072]{1,0:T(8,128)(2,1)} %wqkv_hbm.1, bf16[1024,1024]{1,0:T(8,128)(2,1)} %wout_hbm.1, s32[4,128]{1,0:T(4,128)} %bitcast.5, s32[4,4]{1,0:T(4,128)} %nb_hbm.1, s32[4]{0:T(128)} %cnt_hbm.1), custom_call_target="tpu_custom_call" | custom-call | flops 5000000000 | bytes 12000000 | tf_op jit(solution)/shard_map/pallas_call | solution.py:330
  47.6 1.0 %copy.9 = bf16[1,512,1024]{2,1,0:T(8,128)(2,1)} copy(bf16[1,512,1024]{2,1,0:T(8,128)(2,1)S(1)} %bitcast.3) | data formatting | bytes 2097152

commit v5 on v4

--- a/solution.py
+++ b/solution.py
@@ -240,7 +240,7 @@
         for p in far_first:
             ret_copy(c, peer_of(p), rank).start()
 
-    pl.loop(0, chunks - 1)(temporal)
+    pl.loop(0, chunks)(temporal)
 
     for kind, win in enumerate((kwin, vwin)):
         for side in range(2):
@@ -280,7 +280,6 @@
             jnp.concatenate(outs, axis=1)
         )
 
-    temporal(chunks - 1)
     spatial = dot(place[...], block_out[...]).astype(BF16)
     wout_in.wait()
     for lo in range(0, width, 256):

time: 48.7 us -> 45.9 us (0.943)
  Pallas kernels: 47.6 us -> 44.8 us
    pallas_call x1, Pallas kernels: 47.6 us -> 44.8 us  [body(): pl.pallas_call(functools.partial(kernel, clip), out_shape=jax.ShapeDtypeS...]
where the time goes in v5:
time: 45.9 us; the launch traced here: 45.8 us
  Pallas kernels  44.8 us (98%)
  local copies, waits for them, and re-layouts  0.97 us (2%)
    pallas_call x1, Pallas kernels, body(): pl.pallas_call(functools.partial(kernel, clip), out_shape=jax.ShapeDtypeS...  44.8 us
    unnamed x1, local copies, waits for them, and re-layouts  0.97 us

profile of v5, /device:TPU:0, one launch (start us, length us, event | category | flops | bytes accessed | tf_op | source)
XLA Modules:
  0.0 45.8 jit_solution(7464876295023505108)
XLA Ops:
  0.0 44.8 %shard_map.73 = bf16[8,64,1024]{2,1,0:T(8,128)(2,1)S(1)} custom-call(bf16[8,64,1024]{2,1,0:T(8,128)(2,1)} %bitcast.4, f32[3,1024]{1,0:T(4,128)} %cond_hbm.1, bf16[1024,3072]{1,0:T(8,128)(2,1)} %wqkv_hbm.1, bf16[1024,1024]{1,0:T(8,128)(2,1)} %wout_hbm.1, s32[4,128]{1,0:T(4,128)} %bitcast.5, s32[4,4]{1,0:T(4,128)} %nb_hbm.1, s32[4]{0:T(128)} %cnt_hbm.1), custom_call_target="tpu_custom_call" | custom-call | flops 5000000000 | bytes 12000000 | tf_op jit(solution)/shard_map/pallas_call | solution.py:329
  44.8 1.0 %copy.9 = bf16[1,512,1024]{2,1,0:T(8,128)(2,1)} copy(bf16[1,512,1024]{2,1,0:T(8,128)(2,1)S(1)} %bitcast.3) | data formatting | bytes 2097152

commit v6 on v3

--- a/solution.py
+++ b/solution.py
@@ -211,13 +211,20 @@
         lax.broadcasted_iota(jnp.int32, (rows, rows), 1), CHUNK
     )
 
-    @pl.loop(0, chunks)
-    def _(c):
+    def send_result(c):
+        for p in far_first:
+            ret_copy(c, peer_of(p), rank).start()
+
+    def temporal(c):
         own_copy(c).wait()
 
         @pl.loop(1, clip)
         def _(p):
             lat_copy(c, peer_of(p), peer_of(p)).wait_recv()
+
+        @pl.when(c == chunks - 1)
+        def _():
+            pl.loop(0, chunks - 1)(send_result)
 
         normed = modulate(grp[c].reshape(rows, width), cond_ref)
         q = dot(normed, wqkv[:, half:width]).astype(BF16)
@@ -234,8 +241,8 @@
         t_out[c] = result
         tmp[c, rank] = t_out[c, rank]
 
-        for p in far_first:
-            ret_copy(c, peer_of(p), rank).start()
+    pl.loop(0, chunks)(temporal)
+    send_result(chunks - 1)
 
     for kind, win in enumerate((kwin, vwin)):
         for part in range(2):

time: 45.6 us -> 44.6 us (0.978)
  Pallas kernels: 44.4 us -> 43.5 us
    pallas_call x1, Pallas kernels: 44.4 us -> 43.5 us  [body(): pl.pallas_call(functools.partial(kernel, clip), out_shape=jax.ShapeDtypeS...]
where the time goes in v6:
time: 44.6 us; the launch traced here: 44.4 us
  Pallas kernels  43.5 us (98%)
  local copies, waits for them, and re-layouts  0.97 us (2%)
    pallas_call x1, Pallas kernels, body(): pl.pallas_call(functools.partial(kernel, clip), out_shape=jax.ShapeDtypeS...  43.5 us
    unnamed x1, local copies, waits for them, and re-layouts  0.97 us

profile of v6, /device:TPU:0, one launch (start us, length us, event | category | flops | bytes accessed | tf_op | source)
XLA Modules:
  0.0 44.4 jit_solution(7231274769704140038)
XLA Ops:
  0.0 43.5 %shard_map.73 = bf16[8,64,1024]{2,1,0:T(8,128)(2,1)S(1)} custom-call(bf16[8,64,1024]{2,1,0:T(8,128)(2,1)} %bitcast.4, f32[3,1024]{1,0:T(4,128)} %cond_hbm.1, bf16[1024,3072]{1,0:T(8,128)(2,1)} %wqkv_hbm.1, bf16[1024,1024]{1,0:T(8,128)(2,1)} %wout_hbm.1, s32[4,128]{1,0:T(4,128)} %bitcast.5, s32[4,4]{1,0:T(4,128)} %nb_hbm.1, s32[4]{0:T(128)} %cnt_hbm.1), custom_call_target="tpu_custom_call" | custom-call | flops 5000000000 | bytes 12000000 | tf_op jit(solution)/shard_map/pallas_call | solution.py:327
  43.5 1.0 %copy.9 = bf16[1,512,1024]{2,1,0:T(8,128)(2,1)} copy(bf16[1,512,1024]{2,1,0:T(8,128)(2,1)S(1)} %bitcast.3) | data formatting | bytes 2097152

commit v7 on v6

--- a/solution.py
+++ b/solution.py
@@ -13,7 +13,8 @@
 MESH = pl.DeviceIdType.MESH
 F32 = jnp.float32
 BF16 = jnp.bfloat16
-CHUNK = 16
+CHUNK = 32
+GROUP = 16
 
 
 def modulate(rows, cond_ref):
@@ -50,6 +51,7 @@
     wout,
     grp,
     mod,
+    g_mod,
     ranked,
     query,
     kwin,
@@ -85,6 +87,7 @@
     blocks, block_len = slot_ref.shape
     chunks = per // CHUNK
     rows = clip * CHUNK
+    group_rows = clip * GROUP
     scale = math.log2(math.e) / math.sqrt(head_dim)
 
     far_first = sorted(range(1, clip), key=lambda p: abs(2 * p - clip))
@@ -176,9 +179,8 @@
         copy.wait()
     lat_in.wait()
 
-    @pl.loop(0, clip)
-    def _(i):
-        mod[pl.ds(pl.multiple_of(i * per, per), per), :] = modulate(lat[i], cond_ref)
+    for i in range(clip):
+        mod[i * per : (i + 1) * per, :] = modulate(lat[i], cond_ref)
 
     for b in range(blocks):
         cut = slice(b * block_len, (b + 1) * block_len)
@@ -207,8 +209,9 @@
         part = dot(ranked[...], wqkv[:, lo : lo + 256]).astype(BF16)
         query[:, :, lo : lo + 256] = part.reshape(blocks, block_len, 256)
 
-    same = lax.rem(lax.broadcasted_iota(jnp.int32, (rows, rows), 0), CHUNK) == lax.rem(
-        lax.broadcasted_iota(jnp.int32, (rows, rows), 1), CHUNK
+    square = (group_rows, group_rows)
+    same = lax.rem(lax.broadcasted_iota(jnp.int32, square, 0), GROUP) == lax.rem(
+        lax.broadcasted_iota(jnp.int32, square, 1), GROUP
     )
 
     def send_result(c):
@@ -226,19 +229,24 @@
         def _():
             pl.loop(0, chunks - 1)(send_result)
 
-        normed = modulate(grp[c].reshape(rows, width), cond_ref)
-        q = dot(normed, wqkv[:, half:width]).astype(BF16)
-        k = dot(normed, wqkv[:, width + half : 2 * width]).astype(BF16)
-        v = dot(normed, wqkv[:, 2 * width + half :]).astype(BF16)
-        outs = []
-        for h in range(sheads):
-            cut = slice(h * head_dim, (h + 1) * head_dim)
-            scores = jnp.where(same, dot_t(q[:, cut], k[:, cut]), -jnp.inf)
-            expo = jnp.exp2((scores - jnp.max(scores, axis=-1, keepdims=True)) * scale)
-            total = jnp.sum(expo, axis=-1, keepdims=True)
-            outs.append((dot(expo.astype(BF16), v[:, cut]) / total).astype(BF16))
-        result = jnp.concatenate(outs, axis=1).reshape(clip, CHUNK, half)
-        t_out[c] = result
+        for i in range(clip):
+            g_mod[i * CHUNK : (i + 1) * CHUNK, :] = modulate(grp[c, i], cond_ref)
+        normed = g_mod[...]
+        q, k, v = (
+            dot(normed, wqkv[:, at : at + half]).astype(BF16).reshape(clip, CHUNK, half)
+            for at in (half, width + half, 2 * width + half)
+        )
+        for u in range(0, CHUNK, GROUP):
+            for h in range(sheads):
+                cut = slice(h * head_dim, (h + 1) * head_dim)
+                one_q, one_k, one_v = (
+                    x[:, u : u + GROUP, cut].reshape(group_rows, head_dim) for x in (q, k, v)
+                )
+                scores = jnp.where(same, dot_t(one_q, one_k), -jnp.inf)
+                expo = jnp.exp2((scores - jnp.max(scores, axis=-1, keepdims=True)) * scale)
+                total = jnp.sum(expo, axis=-1, keepdims=True)
+                result = (dot(expo.astype(BF16), one_v) / total).astype(BF16)
+                t_out[c, :, u : u + GROUP, cut] = result.reshape(clip, GROUP, head_dim)
         tmp[c, rank] = t_out[c, rank]
 
     pl.loop(0, chunks)(temporal)
@@ -259,26 +267,21 @@
             at = jnp.where(at >= total_blocks, at - total_blocks, at)
             at = jnp.where(at < 0, at + total_blocks, at)
             ids.append(jnp.clip(at, 0, 3 * blocks - 1))
-        keys = [kwin[at] for at in ids]
-        vals = [vwin[at] for at in ids]
-        q = query[b]
-        outs = []
+        at_rows = pl.ds(pl.multiple_of(b * block_len, block_len), block_len)
         for h in range(sheads):
             cut = slice(h * head_dim, (h + 1) * head_dim)
+            q = query[b, :, cut]
             parts = []
             for n in range(MAXNB):
-                part = dot_t(q[:, cut], keys[n][:, cut])
+                part = dot_t(q, kwin[ids[n], :, cut])
                 if n > 0:
                     part = jnp.where(n < cnt_ref[b], part, -jnp.inf)
                 parts.append(part)
             scores = jnp.concatenate(parts, axis=1)
             expo = jnp.exp2((scores - jnp.max(scores, axis=-1, keepdims=True)) * scale)
             total = jnp.sum(expo, axis=-1, keepdims=True)
-            val = jnp.concatenate([vals[n][:, cut] for n in range(MAXNB)], axis=0)
-            outs.append((dot(expo.astype(BF16), val) / total).astype(BF16))
-        block_out[pl.ds(pl.multiple_of(b * block_len, block_len), block_len), :] = (
-            jnp.concatenate(outs, axis=1)
-        )
+            val = jnp.concatenate([vwin[at, :, cut] for at in ids], axis=0)
+            block_out[at_rows, cut] = (dot(expo.astype(BF16), val) / total).astype(BF16)
 
     spatial = dot(place[...], block_out[...]).astype(BF16)
     wout_in.wait()
@@ -339,6 +342,7 @@
             pltpu.VMEM(w_out.shape, BF16),
             pltpu.VMEM((chunks, clip, CHUNK, width), BF16),
             pltpu.VMEM((tokens, width), BF16),
+            pltpu.VMEM((clip * CHUNK, width), BF16),
             pltpu.VMEM((tokens, width), BF16),
             pltpu.VMEM((blocks, block_len, half), BF16),
             pltpu.VMEM((3 * blocks, block_len, half), BF16),

time: 44.6 us -> 43.4 us (0.973)
  Pallas kernels: 43.5 us -> 42.3 us
    pallas_call x1, Pallas kernels: 43.5 us -> 42.3 us  [body(): pl.pallas_call(functools.partial(kernel, clip), out_shape=jax.ShapeDtypeS...]
where the time goes in v7:
time: 43.4 us; the launch traced here: 43.3 us
  Pallas kernels  42.3 us (97%)
  local copies, waits for them, and re-layouts  0.97 us (2%)
    pallas_call x1, Pallas kernels, body(): pl.pallas_call(functools.partial(kernel, clip), out_shape=jax.ShapeDtypeS...  42.3 us
    unnamed x1, local copies, waits for them, and re-layouts  0.97 us

profile of v7, /device:TPU:0, one launch (start us, length us, event | category | flops | bytes accessed | tf_op | source)
XLA Modules:
  0.0 43.3 jit_solution(13160987204468831679)
XLA Ops:
  0.0 42.3 %shard_map.73 = bf16[8,64,1024]{2,1,0:T(8,128)(2,1)S(1)} custom-call(bf16[8,64,1024]{2,1,0:T(8,128)(2,1)} %bitcast.4, f32[3,1024]{1,0:T(4,128)} %cond_hbm.1, bf16[1024,3072]{1,0:T(8,128)(2,1)} %wqkv_hbm.1, bf16[1024,1024]{1,0:T(8,128)(2,1)} %wout_hbm.1, s32[4,128]{1,0:T(4,128)} %bitcast.5, s32[4,4]{1,0:T(4,128)} %nb_hbm.1, s32[4]{0:T(128)} %cnt_hbm.1), custom_call_target="tpu_custom_call" | custom-call | flops 5000000000 | bytes 12000000 | tf_op jit(solution)/shard_map/pallas_call | solution.py:330
  42.3 1.0 %copy.9 = bf16[1,512,1024]{2,1,0:T(8,128)(2,1)} copy(bf16[1,512,1024]{2,1,0:T(8,128)(2,1)S(1)} %bitcast.3) | data formatting | bytes 2097152

commit v8 on v7

--- a/solution.py
+++ b/solution.py
@@ -63,6 +63,7 @@
     tmp,
     out_v,
     local_sem,
+    w_sem,
     own_sem,
     lat_send,
     lat_recv,
@@ -96,7 +97,10 @@
         return lax.rem(rank + p, clip)
 
     lat_in = pltpu.make_async_copy(lat_hbm, lat, local_sem.at[0])
-    wqkv_in = pltpu.make_async_copy(wqkv_hbm, wqkv, local_sem.at[1])
+    w_in = []
+    for i, at in enumerate((2, 4, 0, 1, 3, 5)):
+        cut = pl.ds(at * half, half)
+        w_in.append(pltpu.make_async_copy(wqkv_hbm.at[:, cut], wqkv.at[:, cut], w_sem.at[i]))
     wout_in = pltpu.make_async_copy(wout_hbm, wout, local_sem.at[2])
     small_in = [
         pltpu.make_async_copy(cond_hbm, cond_ref, local_sem.at[3]),
@@ -160,7 +164,8 @@
     lat_in.start()
     for copy in small_in:
         copy.start()
-    wqkv_in.start()
+    for copy in w_in:
+        copy.start()
 
     @pl.loop(0, chunks)
     def _(c):
@@ -187,27 +192,31 @@
         spots = lax.broadcasted_iota(jnp.int32, (tokens, block_len), 0)
         one_hot = jnp.where(spots == slot_ref[b : b + 1, :], 1.0, 0.0).astype(BF16)
         place[:, cut] = one_hot
-        ranked[cut, :] = lax.dot_general(
+        picked = lax.dot_general(
             one_hot, mod[...], (((0,), (0,)), ((), ())), preferred_element_type=F32
         ).astype(BF16)
-
-    wqkv_in.wait()
-    for kind, win in enumerate((kwin, vwin)):
-        for lo in range(0, half, 256):
-            at = (kind + 1) * width + lo
-            part = dot(ranked[...], wqkv[:, at : at + 256]).astype(BF16)
-            win[blocks : 2 * blocks, :, lo : lo + 256] = part.reshape(blocks, block_len, 256)
-        for part in range(2):
+        ranked[cut, :] = picked
+        if b % 2 == 0:
+            continue
+        two = slice((b - 1) * block_len, (b + 1) * block_len)
+        for kind, win in enumerate((kwin, vwin)):
+            if b == 1:
+                w_in[kind].wait()
+            at = (kind + 1) * width
+            part = dot(ranked[two, :], wqkv[:, at : at + half]).astype(BF16)
+            win[blocks + b - 1 : blocks + b + 1] = part.reshape(2, block_len, half)
             for side in range(2):
-                halo_copy(win, kind, part, side).start()
-            step = 2 * kind + part + 1
-            if step < chunks:
-                send_latent(step)
-    for c in range(5, chunks):
+                halo_copy(win, kind, b // 2, side).start()
+        if (b + 1) // 2 < chunks:
+            send_latent((b + 1) // 2)
+    for c in range(blocks // 2 + 1, chunks):
         send_latent(c)
+    w_in[2].wait()
     for lo in range(0, half, 256):
         part = dot(ranked[...], wqkv[:, lo : lo + 256]).astype(BF16)
         query[:, :, lo : lo + 256] = part.reshape(blocks, block_len, 256)
+    for copy in w_in[3:]:
+        copy.wait()
 
     square = (group_rows, group_rows)
     same = lax.rem(lax.broadcasted_iota(jnp.int32, square, 0), GROUP) == lax.rem(
@@ -354,6 +363,7 @@
             pltpu.VMEM((chunks, clip, CHUNK, half), BF16),
             pltpu.VMEM((clip, per, width), BF16),
             dma((7,)),
+            dma((6,)),
             dma((chunks,)),
             dma((chunks, clip)),
             dma((chunks, clip)),

time: 43.4 us -> 43.5 us (level)
  no operation moved by 1% of the time
where the time goes in v8:
time: 43.5 us; the launch traced here: 43.3 us
  Pallas kernels  42.3 us (97%)
  local copies, waits for them, and re-layouts  0.97 us (2%)
    pallas_call x1, Pallas kernels, body(): pl.pallas_call(functools.partial(kernel, clip), out_shape=jax.ShapeDtypeS...  42.3 us
    unnamed x1, local copies, waits for them, and re-layouts  0.97 us

profile of v8, /device:TPU:0, one launch (start us, length us, event | category | flops | bytes accessed | tf_op | source)
XLA Modules:
  0.0 43.3 jit_solution(14603566558399440709)
XLA Ops:
  0.0 42.3 %shard_map.73 = bf16[8,64,1024]{2,1,0:T(8,128)(2,1)S(1)} custom-call(bf16[8,64,1024]{2,1,0:T(8,128)(2,1)} %bitcast.4, f32[3,1024]{1,0:T(4,128)} %cond_hbm.1, bf16[1024,3072]{1,0:T(8,128)(2,1)} %wqkv_hbm.1, bf16[1024,1024]{1,0:T(8,128)(2,1)} %wout_hbm.1, s32[4,128]{1,0:T(4,128)} %bitcast.5, s32[4,4]{1,0:T(4,128)} %nb_hbm.1, s32[4]{0:T(128)} %cnt_hbm.1), custom_call_target="tpu_custom_call" | custom-call | flops 5000000000 | bytes 12000000 | tf_op jit(solution)/shard_map/pallas_call | solution.py:339
  42.4 1.0 %copy.9 = bf16[1,512,1024]{2,1,0:T(8,128)(2,1)} copy(bf16[1,512,1024]{2,1,0:T(8,128)(2,1)S(1)} %bitcast.3) | data formatting | bytes 2097152

commit v9 on v8

--- a/solution.py
+++ b/solution.py
@@ -41,7 +41,7 @@
     slot_hbm,
     nb_hbm,
     cnt_hbm,
-    out_hbm,
+    out_ref,
     cond_ref,
     slot_ref,
     nb_ref,
@@ -61,7 +61,6 @@
     sp_mixed,
     t_out,
     tmp,
-    out_v,
     local_sem,
     w_sem,
     own_sem,
@@ -71,7 +70,6 @@
     halo_recv,
     ret_send,
     ret_recv,
-    out_sem,
 ):
     space_total = lax.axis_size("space")
     me_s = lax.axis_index("space")
@@ -146,10 +144,6 @@
             device_id={"space": left if side else right},
             device_id_type=MESH,
         )
-
-    def out_copy(c):
-        cut = pl.ds(pl.multiple_of(c * CHUNK, CHUNK), CHUNK)
-        return pltpu.make_async_copy(out_v.at[:, cut], out_hbm.at[:, cut], out_sem.at[c])
 
     barrier = pltpu.get_barrier_semaphore()
 
@@ -230,13 +224,17 @@
     def temporal(c):
         own_copy(c).wait()
 
+        @pl.when(c == chunks - 1)
+        def _():
+            @pl.loop(1, clip)
+            def _(p):
+                lat_copy(c, peer_of(p), rank).wait_send()
+
+            pl.loop(0, chunks - 1)(send_result)
+
         @pl.loop(1, clip)
         def _(p):
             lat_copy(c, peer_of(p), peer_of(p)).wait_recv()
-
-        @pl.when(c == chunks - 1)
-        def _():
-            pl.loop(0, chunks - 1)(send_result)
 
         for i in range(clip):
             g_mod[i * CHUNK : (i + 1) * CHUNK, :] = modulate(grp[c, i], cond_ref)
@@ -308,17 +306,19 @@
         mixed = dot(tmp[c].reshape(rows, half), wout[half:, :]).reshape(clip, CHUNK, width)
         mixed = mixed + sp_mixed[:, cut, :]
         gate = cond_ref[2:3, :].reshape(1, 1, width)
-        out_v[:, cut, :] = (lat[:, cut, :].astype(F32) + gate * mixed).astype(BF16)
-        out_copy(c).start()
+        out_ref[:, cut, :] = (lat[:, cut, :].astype(F32) + gate * mixed).astype(BF16)
 
     @pl.loop(0, chunks)
     def _(c):
-        out_copy(c).wait()
-
+        @pl.loop(1, clip)
+        def _(p):
+            ret_copy(c, peer_of(p), rank).wait_send()
+
+    @pl.loop(0, chunks - 1)
+    def _(c):
         @pl.loop(1, clip)
         def _(p):
             lat_copy(c, peer_of(p), rank).wait_send()
-            ret_copy(c, peer_of(p), rank).wait_send()
 
     for kind, win in enumerate((kwin, vwin)):
         for part in range(2):
@@ -340,7 +340,7 @@
         functools.partial(kernel, clip),
         out_shape=jax.ShapeDtypeStruct((clip, per, width), BF16),
         in_specs=[hbm] * 7,
-        out_specs=hbm,
+        out_specs=pl.BlockSpec(memory_space=pltpu.VMEM),
         scratch_shapes=[
             pltpu.VMEM(cond.shape, F32),
             pltpu.VMEM((blocks, block_len), jnp.int32),
@@ -361,7 +361,6 @@
             pltpu.VMEM((clip, per, width), F32),
             pltpu.VMEM((chunks, clip, CHUNK, half), BF16),
             pltpu.VMEM((chunks, clip, CHUNK, half), BF16),
-            pltpu.VMEM((clip, per, width), BF16),
             dma((7,)),
             dma((6,)),
             dma((chunks,)),
@@ -371,7 +370,6 @@
             dma((2, 2, 2)),
             dma((chunks, clip)),
             dma((chunks, clip)),
-            dma((chunks,)),
         ],
         compiler_params=pltpu.CompilerParams(
             collective_id=0, has_side_effects=True, vmem_limit_bytes=48 * 1024 * 1024

time: 43.5 us -> 44.3 us (1.018)
  Pallas kernels: 42.3 us -> 43.2 us
    pallas_call x1, Pallas kernels: 42.3 us -> 43.2 us  [body(): pl.pallas_call(functools.partial(kernel, clip), out_shape=jax.ShapeDtypeS...]
where the time goes in v9:
time: 44.3 us; the launch traced here: 44.2 us
  Pallas kernels  43.2 us (98%)
  local copies, waits for them, and re-layouts  0.97 us (2%)
    pallas_call x1, Pallas kernels, body(): pl.pallas_call(functools.partial(kernel, clip), out_shape=jax.ShapeDtypeS...  43.2 us
    unnamed x1, local copies, waits for them, and re-layouts  0.97 us

profile of v9, /device:TPU:0, one launch (start us, length us, event | category | flops | bytes accessed | tf_op | source)
XLA Modules:
  0.0 44.2 jit_solution(3283476216308880113)
XLA Ops:
  0.0 43.2 %shard_map.73 = bf16[8,64,1024]{2,1,0:T(8,128)(2,1)S(1)} custom-call(bf16[8,64,1024]{2,1,0:T(8,128)(2,1)} %bitcast.4, f32[3,1024]{1,0:T(4,128)} %cond_hbm.1, bf16[1024,3072]{1,0:T(8,128)(2,1)} %wqkv_hbm.1, bf16[1024,1024]{1,0:T(8,128)(2,1)} %wout_hbm.1, s32[4,128]{1,0:T(4,128)} %bitcast.5, s32[4,4]{1,0:T(4,128)} %nb_hbm.1, s32[4]{0:T(128)} %cnt_hbm.1), custom_call_target="tpu_custom_call" | custom-call | flops 5000000000 | bytes 12000000 | tf_op jit(solution)/shard_map/pallas_call | solution.py:339
  43.2 1.0 %copy.9 = bf16[1,512,1024]{2,1,0:T(8,128)(2,1)} copy(bf16[1,512,1024]{2,1,0:T(8,128)(2,1)S(1)} %bitcast.3) | data formatting | bytes 2097152

commit v10 on v8

--- a/solution.py
+++ b/solution.py
@@ -56,6 +56,8 @@
     query,
     kwin,
     vwin,
+    kfar,
+    vfar,
     place,
     block_out,
     sp_mixed,
@@ -67,8 +69,10 @@
     own_sem,
     lat_send,
     lat_recv,
-    halo_send,
-    halo_recv,
+    near_send,
+    near_recv,
+    far_send,
+    far_recv,
     ret_send,
     ret_recv,
     out_sem,
@@ -136,14 +140,30 @@
             device_id_type=MESH,
         )
 
-    def halo_copy(win, kind, part, side):
-        at = part * (blocks // 2)
+    odd = lax.rem(me_s, 2)
+    near = jnp.where(odd == 1, left, right)
+    far = jnp.where(odd == 1, right, left)
+
+    def in_order(i, count, flip):
+        return jnp.where(flip, count - 1 - i, i)
+
+    def near_copy(win, kind, pair):
         return pltpu.make_async_remote_copy(
-            src_ref=win.at[pl.ds(blocks + at, blocks // 2)],
-            dst_ref=win.at[pl.ds(2 * blocks * side + at, blocks // 2)],
-            send_sem=halo_send.at[kind, part, side],
-            recv_sem=halo_recv.at[kind, part, side],
-            device_id={"space": left if side else right},
+            src_ref=win.at[pl.ds(blocks + 2 * pair, 2)],
+            dst_ref=win.at[pl.ds(2 * blocks * odd + 2 * pair, 2)],
+            send_sem=near_send.at[kind, pair],
+            recv_sem=near_recv.at[kind, pair],
+            device_id={"space": near},
+            device_id_type=MESH,
+        )
+
+    def far_copy(win, land, kind, b):
+        return pltpu.make_async_remote_copy(
+            src_ref=win.at[blocks + b],
+            dst_ref=land.at[b],
+            send_sem=far_send.at[kind, b],
+            recv_sem=far_recv.at[kind, b],
+            device_id={"space": far},
             device_id_type=MESH,
         )
 
@@ -188,27 +208,30 @@
         mod[i * per : (i + 1) * per, :] = modulate(lat[i], cond_ref)
 
     for b in range(blocks):
-        cut = slice(b * block_len, (b + 1) * block_len)
         spots = lax.broadcasted_iota(jnp.int32, (tokens, block_len), 0)
         one_hot = jnp.where(spots == slot_ref[b : b + 1, :], 1.0, 0.0).astype(BF16)
-        place[:, cut] = one_hot
-        picked = lax.dot_general(
-            one_hot, mod[...], (((0,), (0,)), ((), ())), preferred_element_type=F32
+        place[:, b * block_len : (b + 1) * block_len] = one_hot
+    two = 2 * block_len
+    for step in range(blocks // 2):
+        pair = in_order(step, blocks // 2, odd == 1)
+        cut = pl.ds(pl.multiple_of(pair * two, two), two)
+        ranked[cut, :] = lax.dot_general(
+            place[:, cut], mod[...], (((0,), (0,)), ((), ())), preferred_element_type=F32
         ).astype(BF16)
-        ranked[cut, :] = picked
-        if b % 2 == 0:
-            continue
-        two = slice((b - 1) * block_len, (b + 1) * block_len)
         for kind, win in enumerate((kwin, vwin)):
-            if b == 1:
+            if step == 0:
                 w_in[kind].wait()
             at = (kind + 1) * width
-            part = dot(ranked[two, :], wqkv[:, at : at + half]).astype(BF16)
-            win[blocks + b - 1 : blocks + b + 1] = part.reshape(2, block_len, half)
-            for side in range(2):
-                halo_copy(win, kind, b // 2, side).start()
-        if (b + 1) // 2 < chunks:
-            send_latent((b + 1) // 2)
+            part = dot(ranked[cut, :], wqkv[:, at : at + half]).astype(BF16)
+            win[pl.ds(blocks + 2 * pair, 2)] = part.reshape(2, block_len, half)
+        for j in range(2):
+            b = 2 * pair + in_order(j, 2, odd == 1)
+            far_copy(kwin, kfar, 0, b).start()
+            far_copy(vwin, vfar, 1, b).start()
+        near_copy(kwin, 0, pair).start()
+        near_copy(vwin, 1, pair).start()
+        if step + 1 < chunks:
+            send_latent(step + 1)
     for c in range(blocks // 2 + 1, chunks):
         send_latent(c)
     w_in[2].wait()
@@ -262,14 +285,17 @@
     send_result(chunks - 1)
 
     for kind, win in enumerate((kwin, vwin)):
-        for part in range(2):
-            for side in range(2):
-                halo_copy(win, kind, part, side).wait_recv()
+        for pair in range(blocks // 2):
+            near_copy(win, kind, pair).wait_recv()
     first_block = (me_s - 1) * blocks
     total_blocks = blocks * space_total
 
     @pl.loop(0, blocks)
-    def _(b):
+    def _(i):
+        b = in_order(i, blocks, odd == 0)
+        for kind, (win, land) in enumerate(((kwin, kfar), (vwin, vfar))):
+            far_copy(win, land, kind, b).wait_recv()
+            win[2 * blocks * odd + b] = land[b]
         ids = []
         for n in range(MAXNB):
             at = nb_ref[b, n] - first_block
@@ -320,10 +346,11 @@
             lat_copy(c, peer_of(p), rank).wait_send()
             ret_copy(c, peer_of(p), rank).wait_send()
 
-    for kind, win in enumerate((kwin, vwin)):
-        for part in range(2):
-            for side in range(2):
-                halo_copy(win, kind, part, side).wait_send()
+    for kind, (win, land) in enumerate(((kwin, kfar), (vwin, vfar))):
+        for pair in range(blocks // 2):
+            near_copy(win, kind, pair).wait_send()
+        for b in range(blocks):
+            far_copy(win, land, kind, b).wait_send()
 
 
 def body(latent, cond, w_qkv, w_out, slot, neighbours, counts):
@@ -356,6 +383,8 @@
             pltpu.VMEM((blocks, block_len, half), BF16),
             pltpu.VMEM((3 * blocks, block_len, half), BF16),
             pltpu.VMEM((3 * blocks, block_len, half), BF16),
+            pltpu.VMEM((blocks, block_len, half), BF16),
+            pltpu.VMEM((blocks, block_len, half), BF16),
             pltpu.VMEM((tokens, tokens), BF16),
             pltpu.VMEM((tokens, half), BF16),
             pltpu.VMEM((clip, per, width), F32),
@@ -367,8 +396,10 @@
             dma((chunks,)),
             dma((chunks, clip)),
             dma((chunks, clip)),
-            dma((2, 2, 2)),
-            dma((2, 2, 2)),
+            dma((2, blocks // 2)),
+            dma((2, blocks // 2)),
+            dma((2, blocks)),
+            dma((2, blocks)),
             dma((chunks, clip)),
             dma((chunks, clip)),
             dma((chunks,)),

time: 43.5 us -> 43.5 us (level)
  no operation moved by 1% of the time
where the time goes in v10:
time: 43.5 us; the launch traced here: 43.4 us
  Pallas kernels  42.4 us (97%)
  local copies, waits for them, and re-layouts  0.97 us (2%)
    pallas_call x1, Pallas kernels, body(): pl.pallas_call(functools.partial(kernel, clip), out_shape=jax.ShapeDtypeS...  42.4 us
    unnamed x1, local copies, waits for them, and re-layouts  0.97 us

profile of v10, /device:TPU:0, one launch (start us, length us, event | category | flops | bytes accessed | tf_op | source)
XLA Modules:
  0.0 43.4 jit_solution(12227134433061373293)
XLA Ops:
  0.0 42.4 %shard_map.73 = bf16[8,64,1024]{2,1,0:T(8,128)(2,1)S(1)} custom-call(bf16[8,64,1024]{2,1,0:T(8,128)(2,1)} %bitcast.4, f32[3,1024]{1,0:T(4,128)} %cond_hbm.1, bf16[1024,3072]{1,0:T(8,128)(2,1)} %wqkv_hbm.1, bf16[1024,1024]{1,0:T(8,128)(2,1)} %wout_hbm.1, s32[4,128]{1,0:T(4,128)} %bitcast.5, s32[4,4]{1,0:T(4,128)} %nb_hbm.1, s32[4]{0:T(128)} %cnt_hbm.1), custom_call_target="tpu_custom_call" | custom-call | flops 5000000000 | bytes 12000000 | tf_op jit(solution)/shard_map/pallas_call | solution.py:366
  42.4 1.0 %copy.9 = bf16[1,512,1024]{2,1,0:T(8,128)(2,1)} copy(bf16[1,512,1024]{2,1,0:T(8,128)(2,1)S(1)} %bitcast.3) | data formatting | bytes 2097152

commit v11 on v10

--- a/solution.py
+++ b/solution.py
@@ -41,7 +41,7 @@
     slot_hbm,
     nb_hbm,
     cnt_hbm,
-    out_hbm,
+    out_ref,
     cond_ref,
     slot_ref,
     nb_ref,
@@ -63,7 +63,6 @@
     sp_mixed,
     t_out,
     tmp,
-    out_v,
     local_sem,
     w_sem,
     own_sem,
@@ -75,7 +74,6 @@
     far_recv,
     ret_send,
     ret_recv,
-    out_sem,
 ):
     space_total = lax.axis_size("space")
     me_s = lax.axis_index("space")
@@ -166,10 +164,6 @@
             device_id={"space": far},
             device_id_type=MESH,
         )
-
-    def out_copy(c):
-        cut = pl.ds(pl.multiple_of(c * CHUNK, CHUNK), CHUNK)
-        return pltpu.make_async_copy(out_v.at[:, cut], out_hbm.at[:, cut], out_sem.at[c])
 
     barrier = pltpu.get_barrier_semaphore()
 
@@ -334,13 +328,10 @@
         mixed = dot(tmp[c].reshape(rows, half), wout[half:, :]).reshape(clip, CHUNK, width)
         mixed = mixed + sp_mixed[:, cut, :]
         gate = cond_ref[2:3, :].reshape(1, 1, width)
-        out_v[:, cut, :] = (lat[:, cut, :].astype(F32) + gate * mixed).astype(BF16)
-        out_copy(c).start()
+        out_ref[:, cut, :] = (lat[:, cut, :].astype(F32) + gate * mixed).astype(BF16)
 
     @pl.loop(0, chunks)
     def _(c):
-        out_copy(c).wait()
-
         @pl.loop(1, clip)
         def _(p):
             lat_copy(c, peer_of(p), rank).wait_send()
@@ -367,7 +358,7 @@
         functools.partial(kernel, clip),
         out_shape=jax.ShapeDtypeStruct((clip, per, width), BF16),
         in_specs=[hbm] * 7,
-        out_specs=hbm,
+        out_specs=pl.BlockSpec(memory_space=pltpu.VMEM),
         scratch_shapes=[
             pltpu.VMEM(cond.shape, F32),
             pltpu.VMEM((blocks, block_len), jnp.int32),
@@ -390,7 +381,6 @@
             pltpu.VMEM((clip, per, width), F32),
             pltpu.VMEM((chunks, clip, CHUNK, half), BF16),
             pltpu.VMEM((chunks, clip, CHUNK, half), BF16),
-            pltpu.VMEM((clip, per, width), BF16),
             dma((7,)),
             dma((6,)),
             dma((chunks,)),
@@ -402,7 +392,6 @@
             dma((2, blocks)),
             dma((chunks, clip)),
             dma((chunks, clip)),
-            dma((chunks,)),
         ],
         compiler_params=pltpu.CompilerParams(
             collective_id=0, has_side_effects=True, vmem_limit_bytes=48 * 1024 * 1024

time: 43.5 us -> 43.5 us (level)
  no operation moved by 1% of the time
where the time goes in v11:
time: 43.5 us; the launch traced here: 43.3 us
  Pallas kernels  42.4 us (97%)
  local copies, waits for them, and re-layouts  0.97 us (2%)
    pallas_call x1, Pallas kernels, body(): pl.pallas_call(functools.partial(kernel, clip), out_shape=jax.ShapeDtypeS...  42.4 us
    unnamed x1, local copies, waits for them, and re-layouts  0.97 us

profile of v11, /device:TPU:0, one launch (start us, length us, event | category | flops | bytes accessed | tf_op | source)
XLA Modules:
  0.0 43.3 jit_solution(8116378255463034829)
XLA Ops:
  0.0 42.4 %shard_map.73 = bf16[8,64,1024]{2,1,0:T(8,128)(2,1)S(1)} custom-call(bf16[8,64,1024]{2,1,0:T(8,128)(2,1)} %bitcast.4, f32[3,1024]{1,0:T(4,128)} %cond_hbm.1, bf16[1024,3072]{1,0:T(8,128)(2,1)} %wqkv_hbm.1, bf16[1024,1024]{1,0:T(8,128)(2,1)} %wout_hbm.1, s32[4,128]{1,0:T(4,128)} %bitcast.5, s32[4,4]{1,0:T(4,128)} %nb_hbm.1, s32[4]{0:T(128)} %cnt_hbm.1), custom_call_target="tpu_custom_call" | custom-call | flops 5000000000 | bytes 12000000 | tf_op jit(solution)/shard_map/pallas_call | solution.py:357
  42.4 1.0 %copy.9 = bf16[1,512,1024]{2,1,0:T(8,128)(2,1)} copy(bf16[1,512,1024]{2,1,0:T(8,128)(2,1)S(1)} %bitcast.3) | data formatting | bytes 2097152
